TPU v7x, 32 devices: a whole 2x2x4 slice. The times are simulated.
32 devices in a mesh: section: 4 (over y, x), dp: 8 (over z, core).
Axes of the slice: x: 2, y: 2, z: 4, core: 2. Of those that a mesh axis runs over, the one named last changes fastest.
Arguments:
- images_a: bfloat16 [64, 100, 384], P('dp'), may hold values from -6 to 6
- images_b: bfloat16 [64, 196, 384], P('dp'), may hold values from -6 to 6
- images_c: bfloat16 [64, 324, 384], P('dp'), may hold values from -6 to 6
- cotan_a: bfloat16 [64, 100, 384], P('dp'), may hold values from -6 to 6
- cotan_b: bfloat16 [64, 196, 384], P('dp'), may hold values from -6 to 6
- cotan_c: bfloat16 [64, 324, 384], P('dp'), may hold values from -6 to 6
- live_counts: int32 [32, 3], P('dp'), may hold values from 1 to 2, as said below
- scales: bfloat16 [2, 4, 384], replicated, may hold values from 0.25 to 1.75
- shifts: bfloat16 [2, 3, 384], replicated, may hold values from -3 to 3
- mix_a: bfloat16 [2, 100, 100], replicated, may hold values from -0.625 to 0.625
- mix_b: bfloat16 [2, 196, 196], replicated, may hold values from -0.4375 to 0.4375
- mix_c: bfloat16 [2, 324, 324], replicated, may hold values from -0.3125 to 0.3125
- patch_bias: bfloat16 [2, 620], replicated, may hold values from -3 to 3
- weight_in: bfloat16 [2, 384, 1536], replicated, may hold values from -0.3125 to 0.3125
- bias_in: bfloat16 [2, 1536], replicated, may hold values from -3 to 3
- weight_out: bfloat16 [2, 1536, 384], replicated, may hold values from -0.15625 to 0.15625
Outputs:
- output_a: bfloat16 [64, 100, 384], P(('dp', 'section'))
- output_b: bfloat16 [64, 196, 384], P(('dp', 'section'))
- output_c: bfloat16 [64, 324, 384], P(('dp', 'section'))
- grad_a: bfloat16 [64, 100, 384], P(('dp', 'section'))
- grad_b: bfloat16 [64, 196, 384], P(('dp', 'section'))
- grad_c: bfloat16 [64, 324, 384], P(('dp', 'section'))
- grad_scales: float32 [2, 4, 384], replicated
- grad_shifts: float32 [2, 3, 384], replicated
- grad_mix_a: float32 [2, 100, 100], replicated
- grad_mix_b: float32 [2, 196, 196], replicated
- grad_mix_c: float32 [2, 324, 324], replicated
- grad_patch_bias: float32 [2, 620], replicated
- grad_weight_in: float32 [2, 384, 1536], replicated
- grad_bias_in: float32 [2, 1536], replicated
- grad_weight_out: float32 [2, 1536, 384], replicated
Inputs may be any that keep to these rules, and one draw needn't show every extreme that they name: `live_counts`: live images of one size in one micro-batch; some entry is 2 and some is 1.
All inputs are finite; a program needn't handle non-finite values.
Results may differ from a plain program's by a relative error of at most 0.015.
Values may be sent and summed in bfloat16 or wider, within the bound.
A program may use at most 256 MiB of HBM per device.

v0:
```python
import jax
import jax.numpy as jnp
from jax import lax
from jax.sharding import PartitionSpec as P

LAYERS = 2
MICRO = 4
CAP = 2


def for_sending(x):

    def short(part):
        return part.astype(jnp.bfloat16) if part.dtype == jnp.float32 else part

    return jax.tree.map(short, x)


def from_behind(x, axis, by):
    count = lax.axis_size(axis)
    pairs = [(i, i + by) for i in range(count) if 0 <= i + by < count]
    return lax.ppermute(x, axis, pairs)


def body(
    images_a,
    images_b,
    images_c,
    cotan_a,
    cotan_b,
    cotan_c,
    live_counts,
    scales,
    shifts,
    mix_a,
    mix_b,
    mix_c,
    patch_bias,
    weight_in,
    bias_in,
    weight_out,
):
    f32 = jnp.float32
    bf16 = jnp.bfloat16
    section_no = lax.axis_index("section")
    sections = lax.axis_size("section")
    layer_no = section_no // 2
    is_mlp = section_no % 2
    inputs = (images_a, images_b, images_c)
    cotans = (cotan_a, cotan_b, cotan_c)
    widths = tuple((member.shape[1] for member in inputs))
    chans = images_a.shape[2]

    def pick_layer(array):
        return lax.dynamic_index_in_dim(array, layer_no, 0, keepdims=False)

    scale_row = pick_layer(scales).astype(f32)
    shift_row = pick_layer(shifts).astype(f32)
    matrices = (pick_layer(mix_a), pick_layer(mix_b), pick_layer(mix_c))
    bias_row = pick_layer(patch_bias).astype(f32)
    offsets = (
        bias_row[: widths[0]],
        bias_row[widths[0] : widths[0] + widths[1]],
        bias_row[widths[0] + widths[1] :],
    )
    first_weight = pick_layer(weight_in)
    first_bias = pick_layer(bias_in).astype(f32)
    second_weight = pick_layer(weight_out)

    def take_block(array, index):
        return lax.dynamic_slice_in_dim(array, index * CAP, CAP, 0)

    def join_rows(members):
        return jnp.concatenate([member.reshape(-1, member.shape[-1]) for member in members], axis=0)

    def split_rows(joined):
        results = []
        row_start = 0
        for width in widths:
            results.append(joined[row_start : row_start + CAP * width].reshape(CAP, width, chans))
            row_start += CAP * width
        return tuple(results)

    def zero_own():
        return (
            jnp.zeros((7, chans), f32),
            jnp.zeros(matrices[0].shape, f32),
            jnp.zeros(matrices[1].shape, f32),
            jnp.zeros(matrices[2].shape, f32),
            jnp.zeros(bias_row.shape, f32),
            jnp.zeros(first_weight.shape, f32),
            jnp.zeros(first_bias.shape, f32),
            jnp.zeros(second_weight.shape, f32),
        )

    def spare_forward(members):
        return members

    def cross_forward(members):
        results = []
        for member, matrix, offset in zip(members, matrices, offsets):
            source = member.astype(f32)
            normed = (scale_row[0] * source + shift_row[0]).astype(bf16)
            product = jnp.einsum("pq,iqd->ipd", matrix, normed, preferred_element_type=f32)
            results.append((source + scale_row[1] * (product + offset[None, :, None])).astype(bf16))
        return tuple(results)

    def mlp_forward(members):
        joined = join_rows(members).astype(f32)
        normed = (scale_row[2] * joined + shift_row[1]).astype(bf16)
        pre_act = jnp.dot(normed, first_weight, preferred_element_type=f32) + first_bias
        hidden = jax.nn.gelu(pre_act, approximate=False).astype(bf16)
        branch = jnp.dot(hidden, second_weight, preferred_element_type=f32) + shift_row[2]
        return split_rows((joined + scale_row[3] * branch).astype(bf16))

    def spare_backward(members, gradients):
        return (gradients, zero_own())

    def cross_backward(members, gradients):
        gain_grad = jnp.zeros((chans,), f32)
        shift_grad = jnp.zeros((chans,), f32)
        scale_grad = jnp.zeros((chans,), f32)
        mat_grads = []
        off_grads = []
        sent_back = []
        for member, gradient, matrix, offset in zip(members, gradients, matrices, offsets):
            source = member.astype(f32)
            normed = (scale_row[0] * source + shift_row[0]).astype(bf16)
            product = jnp.einsum("pq,iqd->ipd", matrix, normed, preferred_element_type=f32)
            upstream = gradient.astype(f32)
            branch_grad = scale_row[1] * upstream
            rounded = branch_grad.astype(bf16)
            mat_grads.append(jnp.einsum("ipd,iqd->pq", rounded, normed, preferred_element_type=f32))
            off_grads.append(jnp.sum(branch_grad, axis=(0, 2)))
            scale_grad = scale_grad + jnp.sum(
                upstream * (product + offset[None, :, None]), axis=(0, 1)
            )
            normed_grad = jnp.einsum("pq,ipd->iqd", matrix, rounded, preferred_element_type=f32)
            gain_grad = gain_grad + jnp.sum(normed_grad * source, axis=(0, 1))
            shift_grad = shift_grad + jnp.sum(normed_grad, axis=(0, 1))
            sent_back.append((upstream + scale_row[0] * normed_grad).astype(bf16))
        zero_vec = jnp.zeros((chans,), f32)
        vectors = jnp.stack(
            [gain_grad, shift_grad, scale_grad, zero_vec, zero_vec, zero_vec, zero_vec]
        )
        own_grads = (
            vectors,
            mat_grads[0],
            mat_grads[1],
            mat_grads[2],
            jnp.concatenate(off_grads),
            jnp.zeros(first_weight.shape, f32),
            jnp.zeros(first_bias.shape, f32),
            jnp.zeros(second_weight.shape, f32),
        )
        return (tuple(sent_back), own_grads)

    def mlp_backward(members, gradients):
        joined = join_rows(members).astype(f32)
        normed = (scale_row[2] * joined + shift_row[1]).astype(bf16)
        pre_act = jnp.dot(normed, first_weight, preferred_element_type=f32) + first_bias
        hidden = jax.nn.gelu(pre_act, approximate=False).astype(bf16)
        branch = jnp.dot(hidden, second_weight, preferred_element_type=f32) + shift_row[2]
        upstream = join_rows(gradients).astype(f32)
        branch_grad = scale_row[3] * upstream
        rounded = branch_grad.astype(bf16)
        second_grad = jnp.einsum("nh,nd->hd", hidden, rounded, preferred_element_type=f32)
        out_bias_grad = jnp.sum(branch_grad, axis=0)
        scale_grad = jnp.sum(upstream * branch, axis=0)
        hidden_grad = jnp.einsum("nd,hd->nh", rounded, second_weight, preferred_element_type=f32)
        normal_cdf = 0.5 * (1.0 + lax.erf(pre_act * 0.7071067811865476))
        normal_pdf = jnp.exp(-0.5 * pre_act * pre_act) * 0.3989422804014327
        pre_grad = hidden_grad * (normal_cdf + pre_act * normal_pdf)
        pre_rounded = pre_grad.astype(bf16)
        first_grad = jnp.einsum("nd,nh->dh", normed, pre_rounded, preferred_element_type=f32)
        first_bias_grad = jnp.sum(pre_grad, axis=0)
        normed_grad = jnp.einsum("nh,dh->nd", pre_rounded, first_weight, preferred_element_type=f32)
        gain_grad = jnp.sum(normed_grad * joined, axis=0)
        shift_grad = jnp.sum(normed_grad, axis=0)
        sent_back = split_rows((upstream + scale_row[2] * normed_grad).astype(bf16))
        zero_vec = jnp.zeros((chans,), f32)
        vectors = jnp.stack(
            [zero_vec, zero_vec, zero_vec, gain_grad, shift_grad, scale_grad, out_bias_grad]
        )
        own_grads = (
            vectors,
            jnp.zeros(matrices[0].shape, f32),
            jnp.zeros(matrices[1].shape, f32),
            jnp.zeros(matrices[2].shape, f32),
            jnp.zeros(bias_row.shape, f32),
            first_grad,
            first_bias_grad,
            second_grad,
        )
        return (sent_back, own_grads)

    def store(buffer, value, index, is_valid):
        previous = lax.dynamic_index_in_dim(buffer, index, 0, keepdims=False)
        return lax.dynamic_update_index_in_dim(
            buffer, jnp.where(is_valid, value, previous), index, 0
        )

    tick_count = MICRO + sections - 1
    received = tuple((jnp.zeros((CAP, width, chans), bf16) for width in widths))
    kept_inputs = tuple((jnp.zeros((MICRO, CAP, width, chans), bf16) for width in widths))
    finals = tuple((jnp.zeros((MICRO, CAP, width, chans), bf16) for width in widths))
    for moment in range(tick_count):
        micro_no = moment - section_no
        is_valid = (micro_no >= 0) & (micro_no < MICRO)
        safe_index = jnp.clip(micro_no, 0, MICRO - 1)
        fresh_in = tuple((take_block(member, safe_index) for member in inputs))
        current = tuple(
            (
                jnp.where(section_no == 0, fresh_one, recv_one)
                for fresh_one, recv_one in zip(fresh_in, received)
            )
        )
        choose = jnp.where(is_valid, 1 + is_mlp, 0)
        produced = lax.switch(choose, [spare_forward, cross_forward, mlp_forward], current)
        kept_inputs = tuple(
            (
                store(buffer, value, safe_index, is_valid)
                for buffer, value in zip(kept_inputs, current)
            )
        )
        finals = tuple(
            (store(buffer, value, safe_index, is_valid) for buffer, value in zip(finals, produced))
        )
        if moment + 1 < tick_count:
            received = jax.tree.map(
                lambda part, own: part.astype(own.dtype),
                from_behind(for_sending(produced), "section", 1),
                produced,
            )
    slot_ids = jnp.arange(CAP, dtype=jnp.int32)
    totals = zero_own()
    received_back = tuple((jnp.zeros((CAP, width, chans), bf16) for width in widths))
    back_buffer = tuple((jnp.zeros((MICRO, CAP, width, chans), bf16) for width in widths))
    for moment in range(tick_count):
        micro_no = moment - (sections - 1 - section_no)
        is_valid = (micro_no >= 0) & (micro_no < MICRO)
        safe_index = jnp.clip(micro_no, 0, MICRO - 1)
        members = tuple(
            (
                lax.dynamic_index_in_dim(buffer, safe_index, 0, keepdims=False)
                for buffer in kept_inputs
            )
        )
        counts = lax.dynamic_index_in_dim(live_counts, safe_index, 0, keepdims=False)
        fresh_in = tuple(
            (
                take_block(cot_one, safe_index)
                * (slot_ids < counts[kind_no]).astype(bf16)[:, None, None]
                for kind_no, cot_one in enumerate(cotans)
            )
        )
        current = tuple(
            (
                jnp.where(section_no == sections - 1, fresh_one, recv_one)
                for fresh_one, recv_one in zip(fresh_in, received_back)
            )
        )
        choose = jnp.where(is_valid, 1 + is_mlp, 0)
        sent_back, own_grads = lax.switch(
            choose, [spare_backward, cross_backward, mlp_backward], members, current
        )
        totals = jax.tree.map(jnp.add, totals, own_grads)
        back_buffer = tuple(
            (
                store(buffer, value, safe_index, is_valid)
                for buffer, value in zip(back_buffer, sent_back)
            )
        )
        if moment + 1 < tick_count:
            received_back = jax.tree.map(
                lambda part, own: part.astype(own.dtype),
                from_behind(for_sending(sent_back), "section", -1),
                sent_back,
            )
    live_masks = tuple(
        (
            (slot_ids[None, :] < live_counts[:, kind_no][:, None]).astype(bf16)[:, :, None, None]
            for kind_no in range(3)
        )
    )
    shown = tuple((buffer * mask_one for buffer, mask_one in zip(finals, live_masks)))
    per_section = MICRO // sections

    def flatten(members):
        return tuple(
            (
                member.reshape(per_section * CAP, width, chans)
                for member, width in zip(members, widths)
            )
        )

    arrived = (
        lax.all_to_all(for_sending(shown[0]), "section", split_axis=0, concat_axis=0, tiled=True),
        lax.all_to_all(for_sending(shown[1]), "section", split_axis=0, concat_axis=0, tiled=True),
        lax.all_to_all(for_sending(shown[2]), "section", split_axis=0, concat_axis=0, tiled=True),
        lax.all_to_all(
            for_sending(back_buffer[0]), "section", split_axis=0, concat_axis=0, tiled=True
        ),
        lax.all_to_all(
            for_sending(back_buffer[1]), "section", split_axis=0, concat_axis=0, tiled=True
        ),
        lax.all_to_all(
            for_sending(back_buffer[2]), "section", split_axis=0, concat_axis=0, tiled=True
        ),
    )
    last_rows = (sections - 1) * per_section
    kept_out = flatten(
        tuple((member[last_rows : last_rows + per_section] for member in arrived[0:3]))
    )
    kept_back = flatten(tuple((member[0:per_section] for member in arrived[3:6])))
    output_a, output_b, output_c = kept_out
    grad_a, grad_b, grad_c = kept_back
    stacked = lax.psum(
        tuple(
            (
                lax.dynamic_update_index_in_dim(
                    jnp.zeros((LAYERS,) + member.shape, f32), member, layer_no, 0
                )
                for member in totals
            )
        ),
        ("section", "dp"),
    )
    vectors = stacked[0]
    grad_scales = jnp.stack([vectors[:, 0], vectors[:, 2], vectors[:, 3], vectors[:, 5]], axis=1)
    grad_shifts = jnp.stack([vectors[:, 1], vectors[:, 4], vectors[:, 6]], axis=1)
    return (
        output_a,
        output_b,
        output_c,
        grad_a,
        grad_b,
        grad_c,
        grad_scales,
        grad_shifts,
        stacked[1],
        stacked[2],
        stacked[3],
        stacked[4],
        stacked[5],
        stacked[6],
        stacked[7],
    )


def solution(mesh):
    in_specs = (
        P("dp", None, None),
        P("dp", None, None),
        P("dp", None, None),
        P("dp", None, None),
        P("dp", None, None),
        P("dp", None, None),
        P("dp", None),
        P(),
        P(),
        P(),
        P(),
        P(),
        P(),
        P(),
        P(),
        P(),
    )
    out_specs = (
        P(("dp", "section"), None, None),
        P(("dp", "section"), None, None),
        P(("dp", "section"), None, None),
        P(("dp", "section"), None, None),
        P(("dp", "section"), None, None),
        P(("dp", "section"), None, None),
        P(),
        P(),
        P(),
        P(),
        P(),
        P(),
        P(),
        P(),
        P(),
    )
    return jax.shard_map(body, mesh=mesh, in_specs=in_specs, out_specs=out_specs, check_vma=False)
```

profile of v0, /device:TPU:0, one launch (start us, length us, event | category | flops | bytes accessed | tf_op | source)
XLA Modules:
  0.0 1296.3 jit_solution(5366897051024832234)
XLA Ops:
  8.9 4.6 constant_dynamic-slice_fusion.79
  13.5 7.4 constant_dynamic-slice_fusion.78
  21.7 4.6 constant_dynamic-slice_fusion.77
  34.2 15.2 %conditional.14 = ((bf16[2,100,384]{2,1,0:T(8,128)(2,1)}, bf16[2,196,384]{2,1,0:T(8,128)(2,1)S(1)}, bf16[2,324,384]{2,1,0:T(8,128)(2,1)})) conditional(s32[]{:T(128)} %clamp.42, (bf16[2,100,384]{2,1,0:T(8,128)(2,1)}, bf16[2,196,384]{2,1,0:T(8,128)(2,1)S(1)}, bf16[2,324,384]{2,1,0:T(8,128)(2,1)}) %tuple.169, ...), branch_computations={%region_0.1_spmd, %region_1.2_spmd, %region_2.3_spmd} | conditional | flops 3060280320 | bytes 10002464 | solution.py:219
  74.4 5.4 constant_dynamic-slice_fusion.16
  79.8 7.5 constant_dynamic-slice_fusion.14
  87.9 4.6 constant_dynamic-slice_fusion.13
  131.8 10.5 conditional.15
  142.4 23.8 %collective-permute-start.3 = (bf16[2,100,384]{2,1,0:T(8,128)(2,1)}, bf16[2,100,384]{2,1,0:T(8,128)(2,1)S(1)}, u32[]{:S(2)}, u32[]{:S(2)}) collective-permute-start(bf16[2,100,384]{2,1,0:T(8,128)(2,1)} %get-tuple-element.1145), channel_id=1, source_target_pairs={{0,8},{8,16},{16,24},{1,9},{9,17},{17,25},{2,10},{10,18},{18,26},{... | collective-permute-start | bytes 460808 | tf_op jit(solution)/shard_map/ppermute | solution.py:22
  187.7 10.4 conditional.16
  198.1 30.4 %collective-permute-start.6 = (bf16[2,100,384]{2,1,0:T(8,128)(2,1)}, bf16[2,100,384]{2,1,0:T(8,128)(2,1)S(1)}, u32[]{:S(2)}, u32[]{:S(2)}) collective-permute-start(bf16[2,100,384]{2,1,0:T(8,128)(2,1)} %get-tuple-element.1148), channel_id=1, source_target_pairs={{0,8},{8,16},{16,24},{1,9},{9,17},{17,25},{2,10},{10,18},{18,26},{... | collective-permute-start | bytes 460808 | tf_op jit(solution)/shard_map/ppermute | solution.py:22
  250.1 10.7 conditional.17
  260.8 29.8 %collective-permute-start.9 = (bf16[2,100,384]{2,1,0:T(8,128)(2,1)}, bf16[2,100,384]{2,1,0:T(8,128)(2,1)S(1)}, u32[]{:S(2)}, u32[]{:S(2)}) collective-permute-start(bf16[2,100,384]{2,1,0:T(8,128)(2,1)} %get-tuple-element.1151), channel_id=1, source_target_pairs={{0,8},{8,16},{16,24},{1,9},{9,17},{17,25},{2,10},{10,18},{18,26},{... | collective-permute-start | bytes 460808 | tf_op jit(solution)/shard_map/ppermute | solution.py:22
  314.6 38.0 %collective-permute-start.12 = (bf16[2,100,384]{2,1,0:T(8,128)(2,1)}, bf16[2,100,384]{2,1,0:T(8,128)(2,1)S(1)}, u32[]{:S(2)}, u32[]{:S(2)}) collective-permute-start(bf16[2,100,384]{2,1,0:T(8,128)(2,1)} %get-tuple-element.1154), channel_id=1, source_target_pairs={{0,8},{8,16},{16,24},{1,9},{9,17},{17,25},{2,10},{10,18},{18,26},{... | collective-permute-start | bytes 460808 | tf_op jit(solution)/shard_map/ppermute | solution.py:22
  377.5 4.4 collective-permute-start.15
  383.6 10.6 collective-permute-start.16
  413.2 7.6 conditional.20
  423.4 20.1 %all-to-all-start = ((bf16[4,2,100,384]{3,1,2,0:T(2,128)(2,1)}), bf16[4,2,100,384]{3,1,2,0:T(2,128)(2,1)}, u32[]{:S(2)}, u32[]{:S(2)}) async-start(bf16[4,2,100,384]{3,1,2,0:T(2,128)(2,1)} %copy.382), calls=%async_computation | async-start | bytes 1228800 | tf_op jit(solution)/shard_map/all_to_all | solution.py:298
  443.6 13.1 %conditional.21 = (bf16[2,100,384]{2,1,0:T(8,128)(2,1)}, bf16[2,196,384]{2,1,0:T(8,128)(2,1)}, bf16[2,324,384]{2,1,0:T(8,128)(2,1)}, f32[7,384]{1,0:T(8,128)}, f...) conditional(s32[]{:T(128)} %clamp.49, ...), branch_computations={%region_21.22_spmd, %region_22.35_spmd, %region_35.41_spmd} | conditional | flops 8953233408 | bytes 111905920 | solution.py:264
  475.7 49.2 %all-to-all-start.1 = ((bf16[4,2,196,384]{3,1,2,0:T(2,128)(2,1)}), bf16[4,2,196,384]{3,1,2,0:T(2,128)(2,1)}, u32[]{:S(2)}, u32[]{:S(2)}) async-start(bf16[4,2,196,384]{3,1,2,0:T(2,128)(2,1)} %copy.383), calls=%async_computation.1 | async-start | bytes 2408448 | tf_op jit(solution)/shard_map/all_to_all | solution.py:299
  528.7 16.8 %conditional.22 = (bf16[2,100,384]{2,1,0:T(8,128)(2,1)}, bf16[2,196,384]{2,1,0:T(8,128)(2,1)}, bf16[2,324,384]{2,1,0:T(8,128)(2,1)}, f32[7,384]{1,0:T(8,128)}, f...) conditional(s32[]{:T(128)} %clamp.50, ...), branch_computations={%region_41.42_spmd, %region_42.55_spmd, %region_55.61_spmd} | conditional | flops 8953233408 | bytes 113915056 | solution.py:264
  562.4 56.2 %all-to-all-start.2 = ((bf16[4,2,324,384]{3,1,2,0:T(2,128)(2,1)}), bf16[4,2,324,384]{3,1,2,0:T(2,128)(2,1)}, u32[]{:S(2)}, u32[]{:S(2)}) async-start(bf16[4,2,324,384]{3,1,2,0:T(2,128)(2,1)} %copy.384), calls=%async_computation.2 | async-start | bytes 3981312 | tf_op jit(solution)/shard_map/all_to_all | solution.py:300
  622.6 16.8 %conditional.23 = (bf16[2,100,384]{2,1,0:T(8,128)(2,1)}, bf16[2,196,384]{2,1,0:T(8,128)(2,1)}, bf16[2,324,384]{2,1,0:T(8,128)(2,1)}, f32[7,384]{1,0:T(8,128)}, f...) conditional(s32[]{:T(128)} %clamp.51, ...), branch_computations={%region_61.62_spmd, %region_62.75_spmd, %region_75.81_spmd} | conditional | flops 8953233408 | bytes 113915056 | solution.py:264
  651.1 50.7 %collective-permute-done.24 = bf16[2,100,384]{2,1,0:T(8,128)(2,1)S(1)} collective-permute-done((bf16[2,100,384]{2,1,0:T(8,128)(2,1)}, bf16[2,100,384]{2,1,0:T(8,128)(2,1)S(1)}, u32[]{:S(2)}, u32[]{:S(2)}) %collective-permute-start.24) | collective-permute-done | bytes 153632 | tf_op jit(solution)/shard_map/ppermute | solution.py:22
  703.5 5.9 collective-permute-done.25
  710.5 7.7 collective-permute-done.26
  720.3 31.9 %conditional.24 = (bf16[2,100,384]{2,1,0:T(8,128)(2,1)}, bf16[2,196,384]{2,1,0:T(8,128)(2,1)}, bf16[2,324,384]{2,1,0:T(8,128)(2,1)}, f32[7,384]{1,0:T(8,128)}, f...) conditional(s32[]{:T(128)} %clamp.52, ...), branch_computations={%region_81.82_spmd, %region_82.95_spmd, %region_95.101_spmd} | conditional | flops 8953233408 | bytes 114099472 | solution.py:264
  757.5 32.5 %collective-permute-done.27 = bf16[2,100,384]{2,1,0:T(8,128)(2,1)S(1)} collective-permute-done((bf16[2,100,384]{2,1,0:T(8,128)(2,1)}, bf16[2,100,384]{2,1,0:T(8,128)(2,1)S(1)}, u32[]{:S(2)}, u32[]{:S(2)}) %collective-permute-start.27) | collective-permute-done | bytes 153632 | tf_op jit(solution)/shard_map/ppermute | solution.py:22
  791.0 5.6 collective-permute-done.28
  797.6 7.4 collective-permute-done.29
  806.3 31.6 %conditional.25 = (bf16[2,100,384]{2,1,0:T(8,128)(2,1)}, bf16[2,196,384]{2,1,0:T(8,128)(2,1)}, bf16[2,324,384]{2,1,0:T(8,128)(2,1)}, f32[7,384]{1,0:T(8,128)S(1)...) conditional(s32[]{:T(128)} %clamp.53, ...), branch_computations={%region_101.102_spmd, %region_102.115_spmd, %region_115.121_spmd} | conditional | flops 8953233408 | bytes 111733920 | solution.py:264
  843.7 27.6 %collective-permute-done.30 = bf16[2,100,384]{2,1,0:T(8,128)(2,1)S(1)} collective-permute-done((bf16[2,100,384]{2,1,0:T(8,128)(2,1)}, bf16[2,100,384]{2,1,0:T(8,128)(2,1)S(1)}, u32[]{:S(2)}, u32[]{:S(2)}) %collective-permute-start.30) | collective-permute-done | bytes 153632 | tf_op jit(solution)/shard_map/ppermute | solution.py:22
  872.4 5.6 collective-permute-done.31
  879.0 6.7 collective-permute-done.32
  887.0 24.7 %conditional.26 = (bf16[2,100,384]{2,1,0:T(8,128)(2,1)}, bf16[2,196,384]{2,1,0:T(8,128)(2,1)}, bf16[2,324,384]{2,1,0:T(8,128)(2,1)}, f32[7,384]{1,0:T(8,128)}, f...) conditional(s32[]{:T(128)} %clamp.54, ...), branch_computations={%region_121.122_spmd, %region_122.135_spmd, %region_135.141_spmd} | conditional | flops 8953233408 | bytes 113896608 | solution.py:264
  917.3 34.7 %collective-permute-done.33 = bf16[2,100,384]{2,1,0:T(8,128)(2,1)S(1)} collective-permute-done((bf16[2,100,384]{2,1,0:T(8,128)(2,1)}, bf16[2,100,384]{2,1,0:T(8,128)(2,1)S(1)}, u32[]{:S(2)}, u32[]{:S(2)}) %collective-permute-start.33) | collective-permute-done | bytes 153632 | tf_op jit(solution)/shard_map/ppermute | solution.py:22
  953.0 5.6 collective-permute-done.34
  959.6 6.0 collective-permute-done.35
  966.8 33.3 %conditional.27 = (bf16[2,100,384]{2,1,0:T(8,128)(2,1)S(1)}, bf16[2,196,384]{2,1,0:T(8,128)(2,1)S(1)}, bf16[2,324,384]{2,1,0:T(8,128)(2,1)S(1)}, f32[7,384]{1,0:...) conditional(s32[]{:T(128)} %clamp.55, ...), branch_computations={%region_141.142_spmd, %region_142.155_spmd, %region_155.161_spmd} | conditional | flops 8953233408 | bytes 112667680 | solution.py:264
  1007.6 7.8 bitcast_dynamic-update-slice_fusion.1
  1020.1 5.5 dynamic_update_slice.289
  1025.8 6.6 dynamic_update_slice.290
  1034.9 7.9 bitcast_dynamic-update-slice_fusion
  1067.1 5.2 all-to-all-done.3
  1082.6 18.5 %all-to-all-done.4 = bf16[4,2,196,384]{3,1,2,0:T(2,128)(2,1)} async-done(((bf16[4,2,196,384]{3,1,2,0:T(2,128)(2,1)}), bf16[4,2,196,384]{3,1,2,0:T(2,128)(2,1)}, u32[]{:S(2)}, u32[]{:S(2)}) %all-to-all-start.4) | async-done | bytes 1204256 | tf_op jit(solution)/shard_map/all_to_all | solution.py:304
  1106.9 61.1 %all-reduce = (f32[2,7,384]{2,0,1:T(2,128)S(1)}, f32[2,620]{1,0:T(2,128)}, f32[2,1536]{1,0:T(2,128)}) all-reduce(f32[2,7,384]{2,0,1:T(2,128)S(1)} %dynamic_update_slice.287, f32[2,620]{1,0:T(2,128)S(1)} %dynamic_update_slice.291, f32[2,1536]{1,0:T(2,128)S(1)} %dynamic_update_slice.293), channel_id=1, replica_groups=mesh['section'=4,'dp'=8] {'section','dp'}, use_global_device_ids=true, to_apply=%region_161.162 | all-reduce | flops 9688 | bytes 77504 | tf_op jit(solution)/shard_map/psum | solution.py:318
  1173.9 101.9 %all-reduce.4.cloned.1.call-done = (f32[2,100,100]{2,0,1:T(2,128)}, f32[2,196,196]{2,0,1:T(2,128)}, f32[2,324,324]{2,0,1:T(2,128)}, f32[2,384,1536]{2,1,0:T(8,128)}, f32[2,1536,384]{2,1,0:T(8,128)}) async-done(((f32[2,100,100]{2,0,1:T(2,128)}, f32[2,196,196]{2,0,1:T(2,128)}, f32[2,324,324]{2,0,1:T(2,128)}, f32[2,384,1536]{2,1,0:T(8,128)}, f32[2,1536,384]{2,1,0:T(8,128)}), (f32[2,100,100]{2,0,1:T(2,128)}, ...) | async-done | bytes 10664336 | tf_op jit(solution)/shard_map/psum | solution.py:318
  1282.1 4.9 copy.1040
  (738 shorter events, 489.6 us)
Async XLA Ops:
  49.4 74.8 %collective-permute-start = (bf16[2,100,384]{2,1,0:T(8,128)(2,1)}, bf16[2,100,384]{2,1,0:T(8,128)(2,1)}, u32[]{:S(2)}, u32[]{:S(2)}) collective-permute-start(bf16[2,100,384]{2,1,0:T(8,128)(2,1)} %get-tuple-element.1142), channel_id=1, source_target_pairs={{0,8},{8,16},{16,24},{1,9},{9,17},{17,25},{2,10},{10,18},{18,26},{... | collective-permute-start | bytes 460808 | tf_op jit(solution)/shard_map/ppermute | solution.py:22
  51.3 76.3 %collective-permute-start.1 = (bf16[2,196,384]{2,1,0:T(8,128)(2,1)S(1)}, bf16[2,196,384]{2,1,0:T(8,128)(2,1)}, u32[]{:S(2)}, u32[]{:S(2)}) collective-permute-start(bf16[2,196,384]{2,1,0:T(8,128)(2,1)S(1)} %get-tuple-element.1143), channel_id=1, source_target_pairs={{0,8},{8,16},{16,24},{1,9},{9,17},{17,25},{2,10},{10,18},{18,26},{... | collective-permute-start | bytes 903176 | tf_op jit(solution)/shard_map/ppermute | solution.py:22
  53.3 76.2 %collective-permute-start.2 = (bf16[2,324,384]{2,1,0:T(8,128)(2,1)}, bf16[2,324,384]{2,1,0:T(8,128)(2,1)}, u32[]{:S(2)}, u32[]{:S(2)}) collective-permute-start(bf16[2,324,384]{2,1,0:T(8,128)(2,1)} %get-tuple-element.1144), channel_id=1, source_target_pairs={{0,8},{8,16},{16,24},{1,9},{9,17},{17,25},{2,10},{10,18},{18,26},{... | collective-permute-start | bytes 1493000 | tf_op jit(solution)/shard_map/ppermute | solution.py:22
  142.4 38.5 %collective-permute-start.3 = (bf16[2,100,384]{2,1,0:T(8,128)(2,1)}, bf16[2,100,384]{2,1,0:T(8,128)(2,1)S(1)}, u32[]{:S(2)}, u32[]{:S(2)}) collective-permute-start(bf16[2,100,384]{2,1,0:T(8,128)(2,1)} %get-tuple-element.1145), channel_id=1, source_target_pairs={{0,8},{8,16},{16,24},{1,9},{9,17},{17,25},{2,10},{10,18},{18,26},{... | collective-permute-start | bytes 460808 | tf_op jit(solution)/shard_map/ppermute | solution.py:22
  167.9 16.4 %collective-permute-start.4 = (bf16[2,196,384]{2,1,0:T(8,128)(2,1)S(1)}, bf16[2,196,384]{2,1,0:T(8,128)(2,1)S(1)}, u32[]{:S(2)}, u32[]{:S(2)}) collective-permute-start(bf16[2,196,384]{2,1,0:T(8,128)(2,1)S(1)} %get-tuple-element.1146), channel_id=1, source_target_pairs={{0,8},{8,16},{16,24},{1,9},{9,17},{17,25},{2,10},{10,18},{18,26},{... | collective-permute-start | bytes 903176 | tf_op jit(solution)/shard_map/ppermute | solution.py:22
  169.9 16.8 %collective-permute-start.5 = (bf16[2,324,384]{2,1,0:T(8,128)(2,1)}, bf16[2,324,384]{2,1,0:T(8,128)(2,1)S(1)}, u32[]{:S(2)}, u32[]{:S(2)}) collective-permute-start(bf16[2,324,384]{2,1,0:T(8,128)(2,1)} %get-tuple-element.1147), channel_id=1, source_target_pairs={{0,8},{8,16},{16,24},{1,9},{9,17},{17,25},{2,10},{10,18},{18,26},{... | collective-permute-start | bytes 1493000 | tf_op jit(solution)/shard_map/ppermute | solution.py:22
  198.1 45.2 %collective-permute-start.6 = (bf16[2,100,384]{2,1,0:T(8,128)(2,1)}, bf16[2,100,384]{2,1,0:T(8,128)(2,1)S(1)}, u32[]{:S(2)}, u32[]{:S(2)}) collective-permute-start(bf16[2,100,384]{2,1,0:T(8,128)(2,1)} %get-tuple-element.1148), channel_id=1, source_target_pairs={{0,8},{8,16},{16,24},{1,9},{9,17},{17,25},{2,10},{10,18},{18,26},{... | collective-permute-start | bytes 460808 | tf_op jit(solution)/shard_map/ppermute | solution.py:22
  230.2 16.4 %collective-permute-start.7 = (bf16[2,196,384]{2,1,0:T(8,128)(2,1)S(1)}, bf16[2,196,384]{2,1,0:T(8,128)(2,1)S(1)}, u32[]{:S(2)}, u32[]{:S(2)}) collective-permute-start(bf16[2,196,384]{2,1,0:T(8,128)(2,1)S(1)} %get-tuple-element.1149), channel_id=1, source_target_pairs={{0,8},{8,16},{16,24},{1,9},{9,17},{17,25},{2,10},{10,18},{18,26},{... | collective-permute-start | bytes 903176 | tf_op jit(solution)/shard_map/ppermute | solution.py:22
  232.2 16.8 %collective-permute-start.8 = (bf16[2,324,384]{2,1,0:T(8,128)(2,1)}, bf16[2,324,384]{2,1,0:T(8,128)(2,1)S(1)}, u32[]{:S(2)}, u32[]{:S(2)}) collective-permute-start(bf16[2,324,384]{2,1,0:T(8,128)(2,1)} %get-tuple-element.1150), channel_id=1, source_target_pairs={{0,8},{8,16},{16,24},{1,9},{9,17},{17,25},{2,10},{10,18},{18,26},{... | collective-permute-start | bytes 1493000 | tf_op jit(solution)/shard_map/ppermute | solution.py:22
  260.8 44.4 %collective-permute-start.9 = (bf16[2,100,384]{2,1,0:T(8,128)(2,1)}, bf16[2,100,384]{2,1,0:T(8,128)(2,1)S(1)}, u32[]{:S(2)}, u32[]{:S(2)}) collective-permute-start(bf16[2,100,384]{2,1,0:T(8,128)(2,1)} %get-tuple-element.1151), channel_id=1, source_target_pairs={{0,8},{8,16},{16,24},{1,9},{9,17},{17,25},{2,10},{10,18},{18,26},{... | collective-permute-start | bytes 460808 | tf_op jit(solution)/shard_map/ppermute | solution.py:22
  292.2 16.3 %collective-permute-start.10 = (bf16[2,196,384]{2,1,0:T(8,128)(2,1)S(1)}, bf16[2,196,384]{2,1,0:T(8,128)(2,1)S(1)}, u32[]{:S(2)}, u32[]{:S(2)}) collective-permute-start(bf16[2,196,384]{2,1,0:T(8,128)(2,1)S(1)} %get-tuple-element.1152), channel_id=1, source_target_pairs={{0,8},{8,16},{16,24},{1,9},{9,17},{17,25},{2,10},{10,18},{18,26},{... | collective-permute-start | bytes 903176 | tf_op jit(solution)/shard_map/ppermute | solution.py:22
  294.2 16.8 %collective-permute-start.11 = (bf16[2,324,384]{2,1,0:T(8,128)(2,1)}, bf16[2,324,384]{2,1,0:T(8,128)(2,1)S(1)}, u32[]{:S(2)}, u32[]{:S(2)}) collective-permute-start(bf16[2,324,384]{2,1,0:T(8,128)(2,1)} %get-tuple-element.1153), channel_id=1, source_target_pairs={{0,8},{8,16},{16,24},{1,9},{9,17},{17,25},{2,10},{10,18},{18,26},{... | collective-permute-start | bytes 1493000 | tf_op jit(solution)/shard_map/ppermute | solution.py:22
  314.6 52.5 %collective-permute-start.12 = (bf16[2,100,384]{2,1,0:T(8,128)(2,1)}, bf16[2,100,384]{2,1,0:T(8,128)(2,1)S(1)}, u32[]{:S(2)}, u32[]{:S(2)}) collective-permute-start(bf16[2,100,384]{2,1,0:T(8,128)(2,1)} %get-tuple-element.1154), channel_id=1, source_target_pairs={{0,8},{8,16},{16,24},{1,9},{9,17},{17,25},{2,10},{10,18},{18,26},{... | collective-permute-start | bytes 460808 | tf_op jit(solution)/shard_map/ppermute | solution.py:22
  354.2 16.3 %collective-permute-start.13 = (bf16[2,196,384]{2,1,0:T(8,128)(2,1)S(1)}, bf16[2,196,384]{2,1,0:T(8,128)(2,1)S(1)}, u32[]{:S(2)}, u32[]{:S(2)}) collective-permute-start(bf16[2,196,384]{2,1,0:T(8,128)(2,1)S(1)} %get-tuple-element.1155), channel_id=1, source_target_pairs={{0,8},{8,16},{16,24},{1,9},{9,17},{17,25},{2,10},{10,18},{18,26},{... | collective-permute-start | bytes 903176 | tf_op jit(solution)/shard_map/ppermute | solution.py:22
  356.3 16.8 %collective-permute-start.14 = (bf16[2,324,384]{2,1,0:T(8,128)(2,1)}, bf16[2,324,384]{2,1,0:T(8,128)(2,1)S(1)}, u32[]{:S(2)}, u32[]{:S(2)}) collective-permute-start(bf16[2,324,384]{2,1,0:T(8,128)(2,1)} %get-tuple-element.1156), channel_id=1, source_target_pairs={{0,8},{8,16},{16,24},{1,9},{9,17},{17,25},{2,10},{10,18},{18,26},{... | collective-permute-start | bytes 1493000 | tf_op jit(solution)/shard_map/ppermute | solution.py:22
  377.5 27.7 %collective-permute-start.15 = (bf16[2,100,384]{2,1,0:T(8,128)(2,1)}, bf16[2,100,384]{2,1,0:T(8,128)(2,1)S(1)}, u32[]{:S(2)}, u32[]{:S(2)}) collective-permute-start(bf16[2,100,384]{2,1,0:T(8,128)(2,1)} %get-tuple-element.1157), channel_id=1, source_target_pairs={{0,8},{8,16},{16,24},{1,9},{9,17},{17,25},{2,10},{10,18},{18,26},{... | collective-permute-start | bytes 460808 | tf_op jit(solution)/shard_map/ppermute | solution.py:22
  383.6 25.9 %collective-permute-start.16 = (bf16[2,196,384]{2,1,0:T(8,128)(2,1)S(1)}, bf16[2,196,384]{2,1,0:T(8,128)(2,1)S(1)}, u32[]{:S(2)}, u32[]{:S(2)}) collective-permute-start(bf16[2,196,384]{2,1,0:T(8,128)(2,1)S(1)} %get-tuple-element.1158), channel_id=1, source_target_pairs={{0,8},{8,16},{16,24},{1,9},{9,17},{17,25},{2,10},{10,18},{18,26},{... | collective-permute-start | bytes 903176 | tf_op jit(solution)/shard_map/ppermute | solution.py:22
  394.3 16.8 %collective-permute-start.17 = (bf16[2,324,384]{2,1,0:T(8,128)(2,1)}, bf16[2,324,384]{2,1,0:T(8,128)(2,1)S(1)}, u32[]{:S(2)}, u32[]{:S(2)}) collective-permute-start(bf16[2,324,384]{2,1,0:T(8,128)(2,1)} %get-tuple-element.1159), channel_id=1, source_target_pairs={{0,8},{8,16},{16,24},{1,9},{9,17},{17,25},{2,10},{10,18},{18,26},{... | collective-permute-start | bytes 1493000 | tf_op jit(solution)/shard_map/ppermute | solution.py:22
  423.4 52.2 %all-to-all-start = ((bf16[4,2,100,384]{3,1,2,0:T(2,128)(2,1)}), bf16[4,2,100,384]{3,1,2,0:T(2,128)(2,1)}, u32[]{:S(2)}, u32[]{:S(2)}) async-start(bf16[4,2,100,384]{3,1,2,0:T(2,128)(2,1)} %copy.382), calls=%async_computation | async-start | bytes 1228800 | tf_op jit(solution)/shard_map/all_to_all | solution.py:298
  456.7 18.0 %collective-permute-start.18 = (bf16[2,100,384]{2,1,0:T(8,128)(2,1)}, bf16[2,100,384]{2,1,0:T(8,128)(2,1)S(1)}, u32[]{:S(2)}, u32[]{:S(2)}) collective-permute-start(bf16[2,100,384]{2,1,0:T(8,128)(2,1)} %get-tuple-element.1163), channel_id=1, source_target_pairs={{8,0},{16,8},{24,16},{9,1},{17,9},{25,17},{10,2},{18,10},{26,18},{... | collective-permute-start | bytes 460808 | tf_op jit(solution)/shard_map/ppermute | solution.py:22
  458.4 17.1 %collective-permute-start.19 = (bf16[2,196,384]{2,1,0:T(8,128)(2,1)}, bf16[2,196,384]{2,1,0:T(8,128)(2,1)S(1)}, u32[]{:S(2)}, u32[]{:S(2)}) collective-permute-start(bf16[2,196,384]{2,1,0:T(8,128)(2,1)} %get-tuple-element.1164), channel_id=1, source_target_pairs={{8,0},{16,8},{24,16},{9,1},{17,9},{25,17},{10,2},{18,10},{26,18},{... | collective-permute-start | bytes 903176 | tf_op jit(solution)/shard_map/ppermute | solution.py:22
  459.7 66.8 %collective-permute-start.20 = (bf16[2,324,384]{2,1,0:T(8,128)(2,1)}, bf16[2,324,384]{2,1,0:T(8,128)(2,1)}, u32[]{:S(2)}, u32[]{:S(2)}) collective-permute-start(bf16[2,324,384]{2,1,0:T(8,128)(2,1)} %get-tuple-element.1165), channel_id=1, source_target_pairs={{8,0},{16,8},{24,16},{9,1},{17,9},{25,17},{10,2},{18,10},{26,18},{... | collective-permute-start | bytes 1493000 | tf_op jit(solution)/shard_map/ppermute | solution.py:22
  475.7 86.7 %all-to-all-start.1 = ((bf16[4,2,196,384]{3,1,2,0:T(2,128)(2,1)}), bf16[4,2,196,384]{3,1,2,0:T(2,128)(2,1)}, u32[]{:S(2)}, u32[]{:S(2)}) async-start(bf16[4,2,196,384]{3,1,2,0:T(2,128)(2,1)} %copy.383), calls=%async_computation.1 | async-start | bytes 2408448 | tf_op jit(solution)/shard_map/all_to_all | solution.py:299
  545.6 11.1 collective-permute-start.21
  546.9 14.4 %collective-permute-start.22 = (bf16[2,196,384]{2,1,0:T(8,128)(2,1)}, bf16[2,196,384]{2,1,0:T(8,128)(2,1)S(1)}, u32[]{:S(2)}, u32[]{:S(2)}) collective-permute-start(bf16[2,196,384]{2,1,0:T(8,128)(2,1)} %get-tuple-element.1167), channel_id=1, source_target_pairs={{8,0},{16,8},{24,16},{9,1},{17,9},{25,17},{10,2},{18,10},{26,18},{... | collective-permute-start | bytes 903176 | tf_op jit(solution)/shard_map/ppermute | solution.py:22
  548.2 72.3 %collective-permute-start.23 = (bf16[2,324,384]{2,1,0:T(8,128)(2,1)}, bf16[2,324,384]{2,1,0:T(8,128)(2,1)}, u32[]{:S(2)}, u32[]{:S(2)}) collective-permute-start(bf16[2,324,384]{2,1,0:T(8,128)(2,1)} %get-tuple-element.1168), channel_id=1, source_target_pairs={{8,0},{16,8},{24,16},{9,1},{17,9},{25,17},{10,2},{18,10},{26,18},{... | collective-permute-start | bytes 1493000 | tf_op jit(solution)/shard_map/ppermute | solution.py:22
  562.4 483.8 %all-to-all-start.2 = ((bf16[4,2,324,384]{3,1,2,0:T(2,128)(2,1)}), bf16[4,2,324,384]{3,1,2,0:T(2,128)(2,1)}, u32[]{:S(2)}, u32[]{:S(2)}) async-start(bf16[4,2,324,384]{3,1,2,0:T(2,128)(2,1)} %copy.384), calls=%async_computation.2 | async-start | bytes 3981312 | tf_op jit(solution)/shard_map/all_to_all | solution.py:300
  618.6 657.3 %all-reduce.4.cloned.1.call-start = ((), (), s32[]{:S(2)}) async-start(), calls=%async_computation.6 | async-start | bytes 21872640 | tf_op jit(solution)/shard_map/psum | solution.py:318
  639.5 80.8 %copy-start.67 = (f32[196,196]{1,0:T(8,128)}, f32[196,196]{1,0:T(8,128)S(1)}, u32[]{:S(2)}) copy-start(f32[196,196]{1,0:T(8,128)S(1)} %get-tuple-element.1200) | copy-start | bytes 460996
  639.5 80.8 %copy-start.33 = (f32[324,324]{1,0:T(8,128)}, f32[324,324]{1,0:T(8,128)S(1)}, u32[]{:S(2)}) copy-start(f32[324,324]{1,0:T(8,128)S(1)} %get-tuple-element.1207) | copy-start | bytes 1259716
  639.5 80.7 %copy-start.125 = (bf16[1,324,324]{2,1,0:T(8,128)(2,1)S(1)}, bf16[1,324,324]{2,1,0:T(8,128)(2,1)}, u32[]{:S(2)}) copy-start(bf16[1,324,324]{2,1,0:T(8,128)(2,1)} %copy.616) | copy-start | bytes 629860
  639.5 80.7 %copy-start.161 = (bf16[1,196,196]{2,1,0:T(8,128)(2,1)S(1)}, bf16[1,196,196]{2,1,0:T(8,128)(2,1)}, u32[]{:S(2)}) copy-start(bf16[1,196,196]{2,1,0:T(8,128)(2,1)} %copy.617) | copy-start | bytes 230500
  639.5 80.7 %copy-start.211 = (f32[324]{0:T(512)S(1)}, f32[324]{0:T(512)}, u32[]{:S(2)}) copy-start(f32[324]{0:T(512)} %copy-done.209) | copy-start | bytes 3892
  639.5 62.3 %collective-permute-start.24 = (bf16[2,100,384]{2,1,0:T(8,128)(2,1)}, bf16[2,100,384]{2,1,0:T(8,128)(2,1)S(1)}, u32[]{:S(2)}, u32[]{:S(2)}) collective-permute-start(bf16[2,100,384]{2,1,0:T(8,128)(2,1)} %get-tuple-element.1169), channel_id=1, source_target_pairs={{8,0},{16,8},{24,16},{9,1},{17,9},{25,17},{10,2},{18,10},{26,18},{... | collective-permute-start | bytes 460808 | tf_op jit(solution)/shard_map/ppermute | solution.py:22
  642.6 66.8 %collective-permute-start.25 = (bf16[2,196,384]{2,1,0:T(8,128)(2,1)}, bf16[2,196,384]{2,1,0:T(8,128)(2,1)S(1)}, u32[]{:S(2)}, u32[]{:S(2)}) collective-permute-start(bf16[2,196,384]{2,1,0:T(8,128)(2,1)} %get-tuple-element.1170), channel_id=1, source_target_pairs={{8,0},{16,8},{24,16},{9,1},{17,9},{25,17},{10,2},{18,10},{26,18},{... | collective-permute-start | bytes 903176 | tf_op jit(solution)/shard_map/ppermute | solution.py:22
  643.9 74.3 %collective-permute-start.26 = (bf16[2,324,384]{2,1,0:T(8,128)(2,1)}, bf16[2,324,384]{2,1,0:T(8,128)(2,1)S(1)}, u32[]{:S(2)}, u32[]{:S(2)}) collective-permute-start(bf16[2,324,384]{2,1,0:T(8,128)(2,1)} %get-tuple-element.1171), channel_id=1, source_target_pairs={{8,0},{16,8},{24,16},{9,1},{17,9},{25,17},{10,2},{18,10},{26,18},{... | collective-permute-start | bytes 1493000 | tf_op jit(solution)/shard_map/ppermute | solution.py:22
  752.2 37.8 %collective-permute-start.27 = (bf16[2,100,384]{2,1,0:T(8,128)(2,1)}, bf16[2,100,384]{2,1,0:T(8,128)(2,1)S(1)}, u32[]{:S(2)}, u32[]{:S(2)}) collective-permute-start(bf16[2,100,384]{2,1,0:T(8,128)(2,1)} %get-tuple-element.1172), channel_id=1, source_target_pairs={{8,0},{16,8},{24,16},{9,1},{17,9},{25,17},{10,2},{18,10},{26,18},{... | collective-permute-start | bytes 460808 | tf_op jit(solution)/shard_map/ppermute | solution.py:22
  753.5 43.1 %collective-permute-start.28 = (bf16[2,196,384]{2,1,0:T(8,128)(2,1)}, bf16[2,196,384]{2,1,0:T(8,128)(2,1)S(1)}, u32[]{:S(2)}, u32[]{:S(2)}) collective-permute-start(bf16[2,196,384]{2,1,0:T(8,128)(2,1)} %get-tuple-element.1173), channel_id=1, source_target_pairs={{8,0},{16,8},{24,16},{9,1},{17,9},{25,17},{10,2},{18,10},{26,18},{... | collective-permute-start | bytes 903176 | tf_op jit(solution)/shard_map/ppermute | solution.py:22
  754.8 50.3 %collective-permute-start.29 = (bf16[2,324,384]{2,1,0:T(8,128)(2,1)}, bf16[2,324,384]{2,1,0:T(8,128)(2,1)S(1)}, u32[]{:S(2)}, u32[]{:S(2)}) collective-permute-start(bf16[2,324,384]{2,1,0:T(8,128)(2,1)} %get-tuple-element.1174), channel_id=1, source_target_pairs={{8,0},{16,8},{24,16},{9,1},{17,9},{25,17},{10,2},{18,10},{26,18},{... | collective-permute-start | bytes 1493000 | tf_op jit(solution)/shard_map/ppermute | solution.py:22
  838.0 33.4 %collective-permute-start.30 = (bf16[2,100,384]{2,1,0:T(8,128)(2,1)}, bf16[2,100,384]{2,1,0:T(8,128)(2,1)S(1)}, u32[]{:S(2)}, u32[]{:S(2)}) collective-permute-start(bf16[2,100,384]{2,1,0:T(8,128)(2,1)} %get-tuple-element.1175), channel_id=1, source_target_pairs={{8,0},{16,8},{24,16},{9,1},{17,9},{25,17},{10,2},{18,10},{26,18},{... | collective-permute-start | bytes 460808 | tf_op jit(solution)/shard_map/ppermute | solution.py:22
  839.3 38.7 %collective-permute-start.31 = (bf16[2,196,384]{2,1,0:T(8,128)(2,1)}, bf16[2,196,384]{2,1,0:T(8,128)(2,1)S(1)}, u32[]{:S(2)}, u32[]{:S(2)}) collective-permute-start(bf16[2,196,384]{2,1,0:T(8,128)(2,1)} %get-tuple-element.1176), channel_id=1, source_target_pairs={{8,0},{16,8},{24,16},{9,1},{17,9},{25,17},{10,2},{18,10},{26,18},{... | collective-permute-start | bytes 903176 | tf_op jit(solution)/shard_map/ppermute | solution.py:22
  840.6 45.1 %collective-permute-start.32 = (bf16[2,324,384]{2,1,0:T(8,128)(2,1)}, bf16[2,324,384]{2,1,0:T(8,128)(2,1)S(1)}, u32[]{:S(2)}, u32[]{:S(2)}) collective-permute-start(bf16[2,324,384]{2,1,0:T(8,128)(2,1)} %get-tuple-element.1177), channel_id=1, source_target_pairs={{8,0},{16,8},{24,16},{9,1},{17,9},{25,17},{10,2},{18,10},{26,18},{... | collective-permute-start | bytes 1493000 | tf_op jit(solution)/shard_map/ppermute | solution.py:22
  911.7 40.3 %collective-permute-start.33 = (bf16[2,100,384]{2,1,0:T(8,128)(2,1)}, bf16[2,100,384]{2,1,0:T(8,128)(2,1)S(1)}, u32[]{:S(2)}, u32[]{:S(2)}) collective-permute-start(bf16[2,100,384]{2,1,0:T(8,128)(2,1)} %get-tuple-element.1178), channel_id=1, source_target_pairs={{8,0},{16,8},{24,16},{9,1},{17,9},{25,17},{10,2},{18,10},{26,18},{... | collective-permute-start | bytes 460808 | tf_op jit(solution)/shard_map/ppermute | solution.py:22
  913.0 45.6 %collective-permute-start.34 = (bf16[2,196,384]{2,1,0:T(8,128)(2,1)}, bf16[2,196,384]{2,1,0:T(8,128)(2,1)S(1)}, u32[]{:S(2)}, u32[]{:S(2)}) collective-permute-start(bf16[2,196,384]{2,1,0:T(8,128)(2,1)} %get-tuple-element.1179), channel_id=1, source_target_pairs={{8,0},{16,8},{24,16},{9,1},{17,9},{25,17},{10,2},{18,10},{26,18},{... | collective-permute-start | bytes 903176 | tf_op jit(solution)/shard_map/ppermute | solution.py:22
  914.3 51.3 %collective-permute-start.35 = (bf16[2,324,384]{2,1,0:T(8,128)(2,1)}, bf16[2,324,384]{2,1,0:T(8,128)(2,1)S(1)}, u32[]{:S(2)}, u32[]{:S(2)}) collective-permute-start(bf16[2,324,384]{2,1,0:T(8,128)(2,1)} %get-tuple-element.1180), channel_id=1, source_target_pairs={{8,0},{16,8},{24,16},{9,1},{17,9},{25,17},{10,2},{18,10},{26,18},{... | collective-permute-start | bytes 1493000 | tf_op jit(solution)/shard_map/ppermute | solution.py:22
  1059.5 12.8 all-to-all-start.3
  1072.3 28.8 %all-to-all-start.4 = ((bf16[4,2,196,384]{3,1,2,0:T(2,128)(2,1)}), bf16[4,2,196,384]{3,1,2,0:T(2,128)(2,1)}, u32[]{:S(2)}, u32[]{:S(2)}) async-start(bf16[4,2,196,384]{3,1,2,0:T(2,128)(2,1)} %copy.407), calls=%async_computation.4 | async-start | bytes 2408448 | tf_op jit(solution)/shard_map/all_to_all | solution.py:304
  1101.1 71.7 %all-to-all-start.5 = ((bf16[4,2,324,384]{3,1,2,0:T(2,128)(2,1)}), bf16[4,2,324,384]{3,1,2,0:T(2,128)(2,1)S(1)}, u32[]{:S(2)}, u32[]{:S(2)}) async-start(bf16[4,2,324,384]{3,1,2,0:T(2,128)(2,1)} %copy.408), calls=%async_computation.5 | async-start | bytes 3981312 | tf_op jit(solution)/shard_map/all_to_all | solution.py:307
  (124 other events, 2668.1 us)
Sparse Core Ops, SparseCore 0:
  1043.0 232.8 all-reduce.3
where the time goes:
time: 1310 us; the launch traced here: 1300 us
  waiting for transfers between devices  326 us (25%)
  starting transfers between devices  322 us (25%)
  local copies, waits for them, and re-layouts  230 us (18%)
  other arithmetic  178 us (14%)
  loops' own time  84.3 us (6%)
  matrix products  78 us (6%)
  blocking collectives  61.1 us (5%)
  between operations  16.4 us (1%)
    ppermute x36, waiting for transfers between devices, from_behind(): return lax.ppermute(x, axis, pairs)  201 us
    ppermute x36, starting transfers between devices, from_behind(): return lax.ppermute(x, axis, pairs)  184 us
    psum x1, waiting for transfers between devices, body(): lax.psum(tuple((lax.dynamic_update_index_in_dim(jnp.zeros((LAYERS,) + mem...  102 us
    dynamic_update_slice x63, other arithmetic, store(): lax.dynamic_update_index_in_dim(buffer, jnp.where(is_valid, value, previo...  84.5 us
    psum x1, blocking collectives, body(): lax.psum(tuple((lax.dynamic_update_index_in_dim(jnp.zeros((LAYERS,) + mem...  61.1 us
    dynamic_slice x54, local copies, waits for them, and re-layouts, store(): previous = lax.dynamic_index_in_dim(buffer, index, 0, keepdims=False)  60.3 us
    all_to_all x1, starting transfers between devices, body(): lax.all_to_all(for_sending(shown[2]), 'section', split_axis=0, concat_axi...  56.2 us
    another operation x7, loops' own time, body(): lax.switch(choose, [spare_backward, cross_backward, mlp_backward], member...  55.4 us
  transfers between devices with their start and end apart: 43, of which 20 were waited for; matrix products, arithmetic and copies ran while one was open for 31% of the time, Pallas kernels for 0%

commit v1 on v0

v1 whole, which is shorter than its diff:
```python
import functools

import jax
import jax.numpy as jnp
from jax import lax
from jax.experimental import pallas as pl
from jax.experimental.pallas import tpu as pltpu
from jax.sharding import PartitionSpec as P

MESH = pl.DeviceIdType.MESH
f32 = jnp.float32
bf16 = jnp.bfloat16
LAYERS = 2
KINDS = 3
LANES = 128
ROWS = 16
CHUNK = 256
SLACK = 2
BLOCK = 32
HALF_LOG2E = -0.7213475204444817
HALF_ROOT = 0.7071067811865476
PDF_SCALE = 0.3989422804014327


def up(value, unit):
    return -(-value // unit) * unit


def nt(left, right):
    return lax.dot_general(left, right, (((1,), (1,)), ((), ())), preferred_element_type=f32)


def nn(left, right):
    return jnp.dot(left, right, preferred_element_type=f32)


def col_sum(value):
    return jnp.sum(value, axis=0, keepdims=True)


def cuts(total, pieces):
    tiles = total // ROWS
    marks = [tiles * k // pieces * ROWS for k in range(pieces + 1)]
    return [(marks[k], marks[k + 1] - marks[k]) for k in range(pieces)]


class Plan:
    def __init__(self, sections, dp, slots, widths, chans, hid):
        self.sections, self.dp, self.slots, self.widths, self.chans, self.hid = sections, dp, slots, widths, chans, hid
        self.padded = tuple(up(width + 1, ROWS) for width in widths)
        self.wide = tuple(up(rows, LANES) for rows in self.padded)
        self.segments = []
        start = 0
        for kind in range(KINDS):
            for slot in range(slots):
                self.segments.append((kind, slot, start))
                start += self.padded[kind]
        self.rows = start
        self.chunks = hid // CHUNK
        self.steps = self.chunks + 1
        self.pieces = LAYERS * self.steps
        self.depth = min(4, dp // 2)
        self.outer = dp // (2 * self.depth)
        self.size = 2 * chans * CHUNK // LANES
        self.half, self.quarter, self.eighth = self.size // 2, self.size // 4, self.size // 8
        self.last = self.eighth // self.depth
        self.places, place = {}, 0
        for kind in reversed(range(KINDS)):
            self.places[kind] = place
            place += self.padded[kind] * (self.wide[kind] // LANES)
        assert place <= self.size and self.last % ROWS == 0 and sections == 4 and self.depth > 1


def kernel(
    plan,
    xa, xb, xc, ca, cb, cc, counts, scales, shifts, mix_a, mix_b, mix_c, patch_bias, bias_in, w_in_hbm, w_out_hbm,
    oa, ob, oc, ga, gb, gc, result,
    w_in, w_out, pad, pbias, aff, bias32, mat_a, mat_b, mat_c, tam_a, tam_b, tam_c,
    xs, x1s, us, hs, ds, z2, acc, grad, dvr, dvt, z2t, da, vecs, bgrad,
    own, land0, land1, land2, land3,
    io_sem, send_sem, recv_sem,
):
    widths, padded, wide = plan.widths, plan.padded, plan.wide
    slots, chans, rows = plan.slots, plan.chans, plan.rows
    section = lax.axis_index("section")
    dp = lax.axis_index("dp")
    core = lax.rem(dp, 2)
    deep = lax.rem(lax.div(dp, 2), plan.depth)
    block = dp - lax.rem(dp, 2 * plan.depth)
    bit0, bit1 = lax.rem(section, 2), lax.div(section, 2)
    first = jnp.where(core == 0, bit0, bit1)
    second = jnp.where(core == 0, bit1, bit0)
    flip0 = section + 1 - 2 * bit0
    flip1 = section + 2 - 4 * bit1
    first_to = (jnp.where(core == 0, flip0, flip1), dp)
    second_to = (jnp.where(core == 0, flip1, flip0), dp)
    core_to = (section, dp + 1 - 2 * core)

    def deep_to(step):
        return (section, block + lax.rem(deep + step, plan.depth) * 2 + core)

    partners = [core_to, first_to, second_to] + [deep_to(step) for step in range(1, plan.depth)]
    barrier = pltpu.get_barrier_semaphore()
    for partner in partners:
        pl.semaphore_signal(barrier, inc=1, device_id=partner, device_id_type=MESH)

    raw_x, raw_c = (oa, ob, oc), (ga, gb, gc)
    fetches = []
    mine = pl.ds(pl.multiple_of(section * slots, slots), slots)
    pairs = list(zip((xa, xb, xc), raw_x)) + list(zip((ca, cb, cc), raw_c))
    for place, (source, target) in enumerate(pairs):
        fetches.append(pltpu.make_async_copy(source.at[:, mine, :], target, io_sem.at[place]))
    fetches.append(pltpu.make_async_copy(w_in_hbm, w_in, io_sem.at[6]))
    fetches.append(pltpu.make_async_copy(w_out_hbm, w_out, io_sem.at[7]))
    for fetch in fetches[:3] + fetches[6:] + fetches[3:6]:
        fetch.start()

    for layer in range(LAYERS):
        aff[layer, 0:4, :] = scales[layer].astype(f32)
        aff[layer, 4:7, :] = shifts[:, layer, :].astype(f32)
        bias32[layer, :, :] = bias_in[...].astype(f32)[layer : layer + 1]
    pbias[...] = jnp.zeros_like(pbias)
    pbias[0:LAYERS, 0 : patch_bias.shape[1]] = patch_bias[...].astype(f32)
    pad[...] = jnp.zeros_like(pad)

    mats, tams = (mat_a, mat_b, mat_c), (tam_a, tam_b, tam_c)
    offset = 0
    for kind, source in enumerate((mix_a, mix_b, mix_c)):
        width, rows_k, size = widths[kind], padded[kind], wide[kind]
        turned = pltpu.roll(pbias[...], pbias.shape[1] - offset, 1) if offset else pbias[...]
        offset += width
        row = lax.broadcasted_iota(jnp.int32, (size, size), 0)
        col = lax.broadcasted_iota(jnp.int32, (size, size), 1)
        for layer in range(LAYERS):
            pad[0:size, 0:size] = jnp.zeros((size, size), f32)
            pad[0:width, 0:width] = source[:, layer, :].astype(f32)
            biases = turned[layer : layer + 1, 0:size]
            column = jnp.sum(jnp.where(row == col, biases, 0.0), axis=1, keepdims=True)
            whole = jnp.where((col == width) & (row < width), column, pad[0:size, 0:size])
            mats[kind][layer] = whole[0:rows_k, 0:rows_k].astype(bf16)
            tams[kind][layer] = whole.T[0:rows_k, 0:rows_k].astype(bf16)

    def padded_image(value, kind):
        width, rows_k = widths[kind], padded[kind]
        edge = width // 8 * 8
        pad[edge:rows_k, :] = jnp.zeros((rows_k - edge, chans), f32)
        pad[0:width, :] = value
        return pad[0:rows_k, :]

    def live(kind, slot):
        return (slot < counts[section, kind]).astype(f32)

    for kind, slot, start in plan.segments:
        if slot == 0:
            fetches[kind].wait()
        xs[0, pl.ds(start, padded[kind]), :] = padded_image(raw_x[kind][:, slot, :].astype(f32), kind).astype(bf16)

    def ones_row(kind, value):
        row = lax.broadcasted_iota(jnp.int32, value.shape, 0)
        return jnp.where(row == widths[kind], 1.0, value).astype(bf16)

    def forward(layer):
        vec = aff[layer]
        for kind, slot, start in plan.segments:
            span = pl.ds(start, padded[kind])
            x = xs[layer, span, :].astype(f32)
            z = ones_row(kind, vec[0:1] * x + vec[4:5])
            p = nn(mats[kind][layer], z)
            us[layer, span, :] = p.astype(bf16)
            x1 = (x + vec[1:2] * p).astype(bf16)
            x1s[layer, span, :] = x1
            z2[span, :] = (vec[2:3] * x1.astype(f32) + vec[5:6]).astype(bf16)
            if layer < LAYERS - 1:
                acc[span, :] = jnp.broadcast_to(vec[6:7], (padded[kind], chans))

        if layer == 0:
            fetches[6].wait()
            fetches[7].wait()

        for chunk in range(plan.chunks):
            lanes = pl.ds(chunk * CHUNK, CHUNK)
            bias = bias32[layer, :, lanes]
            first_weight = w_in[layer, :, lanes]
            second_weight = w_out[layer, lanes, :]
            for start, size in cuts(rows, 2):
                span = pl.ds(start, size)
                product = nn(z2[span, :], first_weight)
                for low in range(0, size, BLOCK):
                    high = min(low + BLOCK, size)
                    a = product[low:high] + bias
                    cdf = 0.5 + 0.5 * lax.erf(a * HALF_ROOT)
                    slope = a * jnp.exp2(a * a * HALF_LOG2E) * PDF_SCALE
                    block_span = pl.ds(start + low, high - low)
                    hs[layer, chunk, block_span, :] = (a * cdf).astype(bf16)
                    ds[layer, chunk, block_span, :] = (cdf + slope).astype(bf16)
                if layer < LAYERS - 1:
                    acc[span, :] += nn(hs[layer, chunk, span, :], second_weight)

        if layer < LAYERS - 1:
            for kind, slot, start in plan.segments:
                span = pl.ds(start, padded[kind])
                xs[layer + 1, span, :] = (x1s[layer, span, :].astype(f32) + vec[3:4] * acc[span, :]).astype(bf16)

    for layer in range(LAYERS):
        forward(layer)

    for kind, slot, start in plan.segments:
        if slot == 0:
            fetches[KINDS + kind].wait()
        cot = raw_c[kind][:, slot, :].astype(f32) * live(kind, slot)
        grad[pl.ds(start, padded[kind]), :] = padded_image(cot, kind).astype(bf16)

    pl.semaphore_wait(barrier, len(partners))

    base0 = core * plan.half
    base1 = base0 + first * plan.quarter
    base2 = base1 + second * plan.eighth
    base3 = base2 + deep * plan.last

    def at(ref, piece, start, size):
        return ref.at[piece, pl.ds(pl.multiple_of(start, ROWS), size)]

    def send(piece, hop, source, target, to):
        return pltpu.make_async_remote_copy(
            src_ref=source,
            dst_ref=target,
            send_sem=send_sem.at[hop],
            recv_sem=recv_sem.at[piece, hop],
            device_id=to,
            device_id_type=MESH,
        )

    def hop0(piece):
        return [send(piece, 0, at(own, piece, (1 - core) * plan.half, plan.half), land0.at[piece], core_to)]

    def hop1(piece):
        return [send(piece, 1, at(land0, piece, (1 - first) * plan.quarter, plan.quarter), land1.at[piece], first_to)]

    def hop2(piece):
        return [send(piece, 2, at(land1, piece, (1 - second) * plan.eighth, plan.eighth), land2.at[piece], second_to)]

    def hop3(piece):
        return [
            send(
                piece,
                3,
                at(land2, piece, lax.rem(deep + step, plan.depth) * plan.last, plan.last),
                land3.at[piece, step - 1],
                deep_to(step),
            )
            for step in range(1, plan.depth)
        ]

    def hop4(piece):
        spot = at(result, piece, base3, plan.last)
        return [send(piece, 4, spot, spot, deep_to(step)) for step in range(1, plan.depth)]

    def hop5(piece):
        spot = at(result, piece, base2, plan.eighth)
        return [send(piece, 5, spot, spot, second_to)]

    def hop6(piece):
        spot = at(result, piece, base1, plan.quarter)
        return [send(piece, 6, spot, spot, first_to)]

    def hop7(piece):
        spot = at(result, piece, base0, plan.half)
        return [send(piece, 7, spot, spot, core_to)]

    others = plan.last * (plan.depth - 1)

    def brought(piece, hop):
        whole = [
            land0.at[piece],
            land1.at[piece],
            land2.at[piece],
            land3.at[piece],
            at(result, piece, base2, others),
            at(result, piece, base2, plan.eighth),
            at(result, piece, base1, plan.quarter),
            at(result, piece, base0, plan.half),
        ][hop]
        return send(piece, hop, whole, whole, core_to)

    totals = [land0, land1, land2, land3, land3, land2, land1, land0]

    def start(copies):
        for copy in copies:
            copy.start()

    def get(ref, piece, start, size):
        return ref[piece, pl.ds(pl.multiple_of(start, ROWS), size), :].astype(f32)

    def add0(piece):
        land0[piece] = (land0[piece].astype(f32) + get(own, piece, base0, plan.half)).astype(bf16)

    def add1(piece):
        land1[piece] = (land1[piece].astype(f32) + get(land0, piece, first * plan.quarter, plan.quarter)).astype(bf16)

    def add2(piece):
        land2[piece] = (land2[piece].astype(f32) + get(land1, piece, second * plan.eighth, plan.eighth)).astype(bf16)

    def add3(piece):
        total = get(land2, piece, deep * plan.last, plan.last)
        for step in range(plan.depth - 1):
            total = total + land3[piece, step].astype(f32)
        result[piece, pl.ds(pl.multiple_of(base3, ROWS), plan.last), :] = total.astype(bf16)

    def nothing(piece):
        pass

    hops = [hop0, hop1, hop2, hop3, hop4, hop5, hop6, hop7]
    adds = [add0, add1, add2, add3, nothing, nothing, nothing, nothing]

    def tick(moment):
        for stage in range(len(hops) + 1):
            piece = moment - SLACK * stage

            @pl.when((piece >= 0) & (piece < plan.pieces))
            def _(stage=stage, piece=piece):
                if stage > 0:
                    brought(piece, stage - 1).wait_recv()
                    adds[stage - 1](piece)
                if stage < len(hops):
                    start(hops[stage](piece))

    def backward(turn):
        layer = LAYERS - 1 - turn
        vec = aff[layer]
        bias_sum = jnp.zeros((1, chans), f32)
        vecs[...] = jnp.zeros_like(vecs)
        for start in range(0, rows, LANES):
            span = pl.ds(start, min(LANES, rows - start))
            g = grad[span, :].astype(f32)
            dv = vec[3:4] * g
            bias_sum = bias_sum + col_sum(dv)
            low = dv.astype(bf16)
            dvr[span, :] = low
            dvt[:, span] = low.T
            z2t[:, span] = (vec[2:3] * x1s[layer, span, :].astype(f32) + vec[5:6]).astype(bf16).T
            acc[span, :] = jnp.zeros((span.size, chans), f32)

        def step(chunk, carry):
            lanes = pl.ds(pl.multiple_of(chunk * CHUNK, CHUNK), CHUNK)
            first_weight = w_in[layer, :, lanes]
            second_weight = w_out[layer, lanes, :]
            total = jnp.zeros((8, CHUNK), f32)
            for start, size in cuts(rows, 1):
                span = pl.ds(start, size)
                dh = nt(dvr[span, :], second_weight)
                for low in range(0, size, BLOCK):
                    high = min(low + BLOCK, size)
                    block_span = pl.ds(start + low, high - low)
                    dact = dh[low:high] * ds[layer, chunk, block_span, :].astype(f32)
                    total = total + dact.reshape(-1, 8, CHUNK).sum(axis=0)
                    da[block_span, :] = dact.astype(bf16)
                acc[span, :] += nt(da[span, :], first_weight)
            bgrad[:, lanes] = col_sum(total)
            piece = turn * plan.steps + chunk
            gin = nn(z2t[...], da[...]).astype(bf16)
            for part in range(CHUNK // LANES):
                own[piece, pl.ds(part * chans, chans), :] = gin[:, part * LANES : (part + 1) * LANES]
            gout = nn(dvt[...], hs[layer, chunk]).astype(bf16).T
            vecs[...] += (gout.astype(f32) * second_weight.astype(f32)).reshape(-1, 8, chans).sum(axis=0)
            for part in range(chans // LANES):
                own[piece, pl.ds(plan.half + part * CHUNK, CHUNK), :] = gout[:, part * LANES : (part + 1) * LANES]
            tick(piece)
            return carry

        lax.fori_loop(0, plan.chunks, step, 0)

        piece = turn * plan.steps + plan.chunks
        sums = [jnp.zeros((1, chans), f32) for _ in range(5)]
        for kind in range(KINDS):
            width, rows_k, size = widths[kind], padded[kind], wide[kind]
            mix_grad = jnp.zeros((rows_k, rows_k), f32)
            for seg_kind, slot, start in plan.segments:
                if seg_kind != kind:
                    continue
                span = pl.ds(start, rows_k)
                dz2 = acc[span, :]
                sums[3] = sums[3] + col_sum(x1s[layer, span, :].astype(f32) * dz2)
                sums[4] = sums[4] + col_sum(dz2)
                g1 = (grad[span, :].astype(f32) + vec[2:3] * dz2).astype(bf16).astype(f32)
                sums[2] = sums[2] + col_sum(g1 * us[layer, span, :].astype(f32))
                dp = (vec[1:2] * g1).astype(bf16)
                x = xs[layer, span, :].astype(f32)
                z = ones_row(kind, vec[0:1] * x + vec[4:5])
                mix_grad = mix_grad + nt(dp, z)
                dz = nn(tams[kind][layer], dp)
                row = lax.broadcasted_iota(jnp.int32, dz.shape, 0)
                dz = jnp.where(row < width, dz, 0.0)
                sums[0] = sums[0] + col_sum(x * dz)
                sums[1] = sums[1] + col_sum(dz)
                grad[span, :] = (g1 + vec[0:1] * dz).astype(bf16)
            pad[0:rows_k, 0:rows_k] = mix_grad
            if kind == KINDS - 1:
                for place in range(5):
                    pad[width + place : width + place + 1, :] = sums[place]
                pad[width + 5 : width + 6, :] = (col_sum(vecs[...]) + vec[6:7] * bias_sum) / vec[3:4]
                pad[width + 6 : width + 7, :] = bias_sum
                for place in range(plan.hid // chans):
                    spot = width + 7 + place
                    pad[spot : spot + 1, :] = bgrad[:, place * chans : (place + 1) * chans]
            for part in range(size // LANES):
                place = plan.places[kind] + part * rows_k
                own[piece, pl.ds(place, rows_k), :] = pad[0:rows_k, part * LANES : (part + 1) * LANES].astype(bf16)
        tick(piece)

    for turn in range(LAYERS):
        backward(turn)

    def shown(buffer, kind, slot, start):
        return buffer[pl.ds(start, padded[kind]), :].astype(f32)[0 : widths[kind]]

    acc[...] = jnp.zeros_like(acc)

    def drain(moment, carry):
        tick(moment)

        @pl.when(moment == plan.pieces)
        def _():
            for kind, slot, begin in plan.segments:
                raw_c[kind][:, slot, :] = shown(grad, kind, slot, begin).astype(bf16)

        @pl.when(moment < plan.pieces + plan.chunks)
        def _():
            chunk = moment - plan.pieces
            lanes = pl.ds(pl.multiple_of(chunk * CHUNK, CHUNK), CHUNK)
            acc[...] += nn(hs[LAYERS - 1, chunk], w_out[LAYERS - 1, lanes, :])

        @pl.when(moment == plan.pieces + plan.chunks)
        def _():
            vec = aff[LAYERS - 1]
            for kind, slot, begin in plan.segments:
                span = pl.ds(begin, padded[kind])
                y = (x1s[LAYERS - 1, span, :].astype(f32) + vec[3:4] * (acc[span, :] + vec[6:7])).astype(bf16)
                raw_x[kind][:, slot, :] = (y.astype(f32) * live(kind, slot)).astype(bf16)[0 : widths[kind]]

        return carry

    lax.fori_loop(plan.pieces, plan.pieces + SLACK * len(hops), drain, 0)

    for hop, total in enumerate(totals):
        pltpu.make_async_remote_copy(
            src_ref=total,
            dst_ref=total,
            send_sem=send_sem.at[hop],
            recv_sem=recv_sem.at[0, hop],
            device_id=core_to,
            device_id_type=MESH,
        ).wait_send()


def body(plan, *args):
    slots, chans, hid, rows = plan.slots, plan.chans, plan.hid, plan.rows
    images = [(width, slots, chans) for width in plan.widths]
    anywhere = pl.BlockSpec(memory_space=pl.ANY)
    vmem = pl.BlockSpec(memory_space=pltpu.VMEM)
    in_specs = [anywhere] * 6 + [pl.BlockSpec(memory_space=pltpu.SMEM)] + [vmem] * 7 + [anywhere] * 2
    (
        *pictures,
        live_counts,
        scales,
        shifts,
        mix_a,
        mix_b,
        mix_c,
        patch_bias,
        weight_in,
        bias_in,
        weight_out,
    ) = args
    scratch = [
        pltpu.VMEM((LAYERS, chans, hid), bf16),
        pltpu.VMEM((LAYERS, hid, chans), bf16),
        pltpu.VMEM((max(plan.wide), chans), f32),
        pltpu.VMEM((8, up(patch_bias.shape[1], LANES)), f32),
        pltpu.VMEM((LAYERS, 8, chans), f32),
        pltpu.VMEM((LAYERS, 1, hid), f32),
    ]
    scratch += [pltpu.VMEM((LAYERS, size, size), bf16) for size in plan.padded * 2]
    scratch += [
        pltpu.VMEM((LAYERS, rows, chans), bf16),
        pltpu.VMEM((LAYERS, rows, chans), bf16),
        pltpu.VMEM((LAYERS, rows, chans), bf16),
        pltpu.VMEM((LAYERS, plan.chunks, rows, CHUNK), bf16),
        pltpu.VMEM((LAYERS, plan.chunks, rows, CHUNK), bf16),
        pltpu.VMEM((rows, chans), bf16),
        pltpu.VMEM((rows, chans), f32),
        pltpu.VMEM((rows, chans), bf16),
        pltpu.VMEM((rows, chans), bf16),
        pltpu.VMEM((chans, rows), bf16),
        pltpu.VMEM((chans, rows), bf16),
        pltpu.VMEM((rows, CHUNK), bf16),
        pltpu.VMEM((8, chans), f32),
        pltpu.VMEM((1, hid), f32),
        pltpu.VMEM((plan.pieces, plan.size, LANES), bf16),
        pltpu.VMEM((plan.pieces, plan.half, LANES), bf16),
        pltpu.VMEM((plan.pieces, plan.quarter, LANES), bf16),
        pltpu.VMEM((plan.pieces, plan.eighth, LANES), bf16),
        pltpu.VMEM((plan.pieces, plan.depth - 1, plan.last, LANES), bf16),
        pltpu.SemaphoreType.DMA((8,)),
        pltpu.SemaphoreType.DMA((8,)),
        pltpu.SemaphoreType.DMA((plan.pieces, 8)),
    ]
    out_shape = [pltpu.VMEM(shape, bf16) for shape in images * 2]
    stays = pltpu.VMEM if plan.outer == 1 else jax.ShapeDtypeStruct
    out_shape.append(stays((plan.pieces, plan.size, LANES), bf16))
    views = [picture.transpose(1, 0, 2) for picture in pictures]
    mixes = [mix.transpose(1, 0, 2) for mix in (mix_a, mix_b, mix_c)]
    *shown, sums = pl.pallas_call(
        functools.partial(kernel, plan),
        out_shape=out_shape,
        in_specs=in_specs,
        out_specs=[vmem] * 7,
        scratch_shapes=scratch,
        compiler_params=pltpu.CompilerParams(
            collective_id=0, has_side_effects=True, vmem_limit_bytes=(55 if plan.outer == 1 else 60) * 1024 * 1024
        ),
    )(*views, live_counts, scales, shifts.transpose(1, 0, 2), *mixes, patch_bias, bias_in, weight_in, weight_out)
    if plan.outer > 1:
        ring = 2 * plan.depth
        groups = [[low + ring * high for high in range(plan.outer)] for low in range(ring)]
        sums = lax.psum(sums, "dp", axis_index_groups=groups)
    finals = [jax.ShapeDtypeStruct(shape, bf16) for shape in images * 2]
    finals += [
        jax.ShapeDtypeStruct(shape, f32)
        for shape in [(LAYERS, 4, chans), (3, LAYERS, chans)]
        + [(width, LAYERS, width) for width in plan.widths]
        + [(LAYERS, sum(plan.widths)), (LAYERS, chans, hid), (LAYERS, hid), (LAYERS, hid, chans)]
    ]
    out = pl.pallas_call(
        functools.partial(unpack, plan),
        out_shape=finals,
        in_specs=[vmem] * 7,
        out_specs=[anywhere] * 6 + [vmem] * 6 + [anywhere, vmem, anywhere],
        scratch_shapes=[
            pltpu.VMEM((LAYERS, chans, hid), f32),
            pltpu.VMEM((LAYERS, hid, chans), f32),
            pltpu.VMEM((max(plan.wide), chans), f32),
            pltpu.SemaphoreType.DMA((6,)),
            pltpu.SemaphoreType.DMA((LAYERS, plan.chunks, 2)),
        ],
        compiler_params=pltpu.CompilerParams(vmem_limit_bytes=24 * 1024 * 1024),
    )(*shown, sums)
    order = [value.transpose(1, 0, 2) for value in out[:6]]
    return (*order, out[6], out[7].transpose(1, 0, 2), *(mix.transpose(1, 0, 2) for mix in out[8:11]), *out[11:])


def unpack(
    plan, ia, ib, ic, ja, jb, jc, held,
    oa, ob, oc, ga, gb, gc, g_scales, g_shifts, g_mix_a, g_mix_b, g_mix_c, g_patch, g_in, g_bias, g_out,
    wide_in, wide_out, square, copy_sem, out_sem,
):
    chans, chunks = plan.chans, plan.chunks
    moves = []
    for place, (source, target) in enumerate(zip((ia, ib, ic, ja, jb, jc), (oa, ob, oc, ga, gb, gc))):
        moves.append(pltpu.make_async_copy(source, target, copy_sem.at[place]))
    g_patch[...] = jnp.zeros_like(g_patch)
    for layer in reversed(range(LAYERS)):
        if layer == 0:
            for move in moves[:6]:
                move.start()
        first = (LAYERS - 1 - layer) * plan.steps
        for step in range(chunks):
            lanes = pl.ds(step * CHUNK, CHUNK)
            for part in range(CHUNK // LANES):
                spot = pl.ds(step * CHUNK + part * LANES, LANES)
                wide_in[layer, :, spot] = held[first + step, pl.ds(part * chans, chans), :].astype(f32)
            for part in range(chans // LANES):
                spot = pl.ds(part * LANES, LANES)
                wide_out[layer, lanes, spot] = held[first + step, pl.ds(plan.half + part * CHUNK, CHUNK), :].astype(f32)
            for place, (source, target) in enumerate(
                ((wide_in.at[layer, :, lanes], g_in.at[layer, :, lanes]), (wide_out.at[layer, lanes], g_out.at[layer, lanes]))
            ):
                moves.append(pltpu.make_async_copy(source, target, out_sem.at[layer, step, place]))
                moves[-1].start()
        offset = 0
        for kind, target in enumerate((g_mix_a, g_mix_b, g_mix_c)):
            width, rows_k, size = plan.widths[kind], plan.padded[kind], plan.wide[kind]
            for part in range(size // LANES):
                place = plan.places[kind] + part * rows_k
                square[0:rows_k, part * LANES : (part + 1) * LANES] = held[first + chunks, pl.ds(place, rows_k), :].astype(
                    f32
                )
            whole = square[0:rows_k, 0:size]
            target[:, layer, :] = whole[0:width, 0:width]
            row = lax.broadcasted_iota(jnp.int32, (rows_k, size), 0)
            col = lax.broadcasted_iota(jnp.int32, (rows_k, size), 1)
            column = jnp.sum(jnp.where(col == width, whole, 0.0), axis=1, keepdims=True)
            turned = jnp.sum(jnp.where((row == col) & (row < width), column, 0.0), axis=0, keepdims=True)
            g_patch[layer : layer + 1, offset : offset + width] = turned[:, 0:width]
            offset += width
        small = square[width : width + 7 + plan.hid // chans, :]
        for place, row in enumerate((0, 2, 3, 5)):
            g_scales[layer, place : place + 1, :] = small[row : row + 1]
        for place, row in enumerate((1, 4, 6)):
            g_shifts[place, layer : layer + 1, :] = small[row : row + 1]
        for place in range(plan.hid // chans):
            g_bias[layer : layer + 1, place * chans : (place + 1) * chans] = small[7 + place : 8 + place]
    for move in moves:
        move.wait()


def solution(mesh):
    sections, dp = mesh.shape["section"], mesh.shape["dp"]

    def run(*args):
        images, weight_in = args[:3], args[13]
        slots = images[0].shape[0] // (sections * dp)
        widths = tuple(image.shape[1] for image in images)
        plan = Plan(sections, dp, slots, widths, weight_in.shape[1], weight_in.shape[2])
        split_in = P("dp", None, None)
        split_out = P(("dp", "section"), None, None)
        in_specs = (split_in,) * 6 + (P("dp", None),) + (P(),) * 9
        out_specs = (split_out,) * 6 + (P(),) * 9
        whole = jax.shard_map(
            functools.partial(body, plan), mesh=mesh, in_specs=in_specs, out_specs=out_specs, check_vma=False
        )
        return whole(*args)

    return run
```

time: 1310 us -> 94.7 us (0.07); the launches traced: 1300 us -> 94.6 us
  waiting for transfers between devices: 326 us -> 0 us
  starting transfers between devices: 322 us -> 0 us
  local copies, waits for them, and re-layouts: 230 us -> 0 us
  other arithmetic: 178 us -> 0 us
  Pallas kernels: 0 us -> 93.7 us
  loops' own time: 84.3 us -> 0 us
  matrix products: 78 us -> 0 us
  blocking collectives: 61.1 us -> 0 us
  between operations: 16.4 us -> 0.82 us
    ppermute x36 -> x0, waiting for transfers between devices: 201 us -> none  [from_behind(): return lax.ppermute(x, axis, pairs)]
    ppermute x36 -> x0, starting transfers between devices: 184 us -> none  [from_behind(): return lax.ppermute(x, axis, pairs)]
    all_to_all x6 -> x0, starting transfers between devices: 138 us -> none  [the longest x1 56.2 us: body(): lax.all_to_all(for_sending(shown[2]), 'section', split_axis=0, concat_axi...]
    psum x1 -> x0, waiting for transfers between devices: 102 us -> none  [body(): lax.psum(tuple((lax.dynamic_update_index_in_dim(jnp.zeros((LAYERS,) + mem...]
    dynamic_update_slice x65 -> x0, other arithmetic: 100 us -> none  [the longest x63 84.5 us: store(): lax.dynamic_update_index_in_dim(buffer, jnp.where(is_valid, value, previo...]
    dynamic_slice x65 -> x0, local copies, waits for them, and re-layouts: 95.8 us -> none  [the longest x54 60.3 us: store(): previous = lax.dynamic_index_in_dim(buffer, index, 0, keepdims=False)]
    pallas_call x0 -> x2, Pallas kernels: none -> 93.7 us  [the longest x1 87.6 us: body(): pl.pallas_call(functools.partial(kernel, plan), out_shape=out_shape, in_s...]
    another operation x14 -> x0, loops' own time: 84.3 us -> none  [the longest x7 55.4 us: body(): lax.switch(choose, [spare_backward, cross_backward, mlp_backward], member...]
  transfers between devices with their start and end apart: 43 -> 0, of which waited for: 20 -> 0; matrix products, arithmetic and copies ran while one was open for 31% -> 0% of each run, Pallas kernels for 0% -> 0%
where the time goes in v1:
time: 94.7 us; the launch traced here: 94.6 us
  Pallas kernels  93.7 us (99%)
    pallas_call x1, Pallas kernels, body(): pl.pallas_call(functools.partial(kernel, plan), out_shape=out_shape, in_s...  87.6 us
    pallas_call x1, Pallas kernels, body(): pl.pallas_call(functools.partial(unpack, plan), out_shape=finals, in_spec...  6.17 us

profile of v1, /device:TPU:0, one launch (start us, length us, event | category | flops | bytes accessed | tf_op | source)
XLA Modules:
  0.0 94.6 jit_solution(3788209457989506599)
XLA Ops:
  0.7 87.6 %shard_map.271 = (bf16[100,2,384]{2,1,0:T(2,128)(2,1)S(1)}, bf16[196,2,384]{2,1,0:T(2,128)(2,1)S(1)}, bf16[324,2,384]{2,1,0:T(2,128)(2,1)S(1)}, bf16[100,2,384]{...) custom-call(bf16[100,8,384]{2,1,0:T(8,128)(2,1)} %bitcast.24, ...), custom_call_target="tpu_custom_call" | custom-call | tf_op jit(solution)/shard_map/pallas_call | solution.py:512
  88.2 6.2 %shard_map.272 = (bf16[100,2,384]{2,1,0:T(2,128)(2,1)}, bf16[196,2,384]{2,1,0:T(2,128)(2,1)}, bf16[324,2,384]{2,1,0:T(2,128)(2,1)}, bf16[100,2,384]{2,1,0:T(2,12...) custom-call(bf16[100,2,384]{2,1,0:T(2,128)(2,1)S(1)} %get-tuple-elem, ...), custom_call_target="tpu_custom_call" | custom-call | tf_op jit(solution)/shard_map/pallas_call | solution.py:533

commit v2 on v1

--- a/solution.py
+++ b/solution.py
@@ -155,23 +155,38 @@
             fetches[kind].wait()
         xs[0, pl.ds(start, padded[kind]), :] = padded_image(raw_x[kind][:, slot, :].astype(f32), kind).astype(bf16)
 
-    def ones_row(kind, value):
-        row = lax.broadcasted_iota(jnp.int32, value.shape, 0)
-        return jnp.where(row == widths[kind], 1.0, value).astype(bf16)
+    def blocks(kind):
+        return [(low, min(BLOCK, padded[kind] - low)) for low in range(0, padded[kind], BLOCK)]
+
+    def rows_from(low, shape):
+        return lax.broadcasted_iota(jnp.int32, shape, 0) + low
+
+    def mixer_input(kind, low, x, vec):
+        z = vec[0:1] * x + vec[4:5]
+        if low <= widths[kind] < low + x.shape[0]:
+            z = jnp.where(rows_from(low, z.shape) == widths[kind], 1.0, z)
+        return z.astype(bf16)
+
+    def fold(value):
+        return value.reshape(-1, 8, chans).sum(axis=0)
 
     def forward(layer):
         vec = aff[layer]
         for kind, slot, start in plan.segments:
             span = pl.ds(start, padded[kind])
-            x = xs[layer, span, :].astype(f32)
-            z = ones_row(kind, vec[0:1] * x + vec[4:5])
-            p = nn(mats[kind][layer], z)
-            us[layer, span, :] = p.astype(bf16)
-            x1 = (x + vec[1:2] * p).astype(bf16)
-            x1s[layer, span, :] = x1
-            z2[span, :] = (vec[2:3] * x1.astype(f32) + vec[5:6]).astype(bf16)
-            if layer < LAYERS - 1:
-                acc[span, :] = jnp.broadcast_to(vec[6:7], (padded[kind], chans))
+            for low, size in blocks(kind):
+                part = pl.ds(start + low, size)
+                z2[part, :] = mixer_input(kind, low, xs[layer, part, :].astype(f32), vec)
+            product = nn(mats[kind][layer], z2[span, :])
+            for low, size in blocks(kind):
+                part = pl.ds(start + low, size)
+                p = product[low : low + size]
+                us[layer, part, :] = p.astype(bf16)
+                x1 = (xs[layer, part, :].astype(f32) + vec[1:2] * p).astype(bf16)
+                x1s[layer, part, :] = x1
+                z2[part, :] = (vec[2:3] * x1.astype(f32) + vec[5:6]).astype(bf16)
+                if layer < LAYERS - 1:
+                    acc[part, :] = jnp.broadcast_to(vec[6:7], (size, chans))
 
         if layer == 0:
             fetches[6].wait()
@@ -182,7 +197,7 @@
             bias = bias32[layer, :, lanes]
             first_weight = w_in[layer, :, lanes]
             second_weight = w_out[layer, lanes, :]
-            for start, size in cuts(rows, 2):
+            for start, size in cuts(rows, 4):
                 span = pl.ds(start, size)
                 product = nn(z2[span, :], first_weight)
                 for low in range(0, size, BLOCK):
@@ -345,7 +360,7 @@
             first_weight = w_in[layer, :, lanes]
             second_weight = w_out[layer, lanes, :]
             total = jnp.zeros((8, CHUNK), f32)
-            for start, size in cuts(rows, 1):
+            for start, size in cuts(rows, 4):
                 span = pl.ds(start, size)
                 dh = nt(dvr[span, :], second_weight)
                 for low in range(0, size, BLOCK):
@@ -370,7 +385,7 @@
         lax.fori_loop(0, plan.chunks, step, 0)
 
         piece = turn * plan.steps + plan.chunks
-        sums = [jnp.zeros((1, chans), f32) for _ in range(5)]
+        sums = [jnp.zeros((8, chans), f32) for _ in range(5)]
         for kind in range(KINDS):
             width, rows_k, size = widths[kind], padded[kind], wide[kind]
             mix_grad = jnp.zeros((rows_k, rows_k), f32)
@@ -378,25 +393,31 @@
                 if seg_kind != kind:
                     continue
                 span = pl.ds(start, rows_k)
-                dz2 = acc[span, :]
-                sums[3] = sums[3] + col_sum(x1s[layer, span, :].astype(f32) * dz2)
-                sums[4] = sums[4] + col_sum(dz2)
-                g1 = (grad[span, :].astype(f32) + vec[2:3] * dz2).astype(bf16).astype(f32)
-                sums[2] = sums[2] + col_sum(g1 * us[layer, span, :].astype(f32))
-                dp = (vec[1:2] * g1).astype(bf16)
-                x = xs[layer, span, :].astype(f32)
-                z = ones_row(kind, vec[0:1] * x + vec[4:5])
-                mix_grad = mix_grad + nt(dp, z)
-                dz = nn(tams[kind][layer], dp)
-                row = lax.broadcasted_iota(jnp.int32, dz.shape, 0)
-                dz = jnp.where(row < width, dz, 0.0)
-                sums[0] = sums[0] + col_sum(x * dz)
-                sums[1] = sums[1] + col_sum(dz)
-                grad[span, :] = (g1 + vec[0:1] * dz).astype(bf16)
+                for low, count in blocks(kind):
+                    part = pl.ds(start + low, count)
+                    dz2 = acc[part, :]
+                    sums[3] = sums[3] + fold(x1s[layer, part, :].astype(f32) * dz2)
+                    sums[4] = sums[4] + fold(dz2)
+                    low_g = (grad[part, :].astype(f32) + vec[2:3] * dz2).astype(bf16)
+                    grad[part, :] = low_g
+                    g1 = low_g.astype(f32)
+                    sums[2] = sums[2] + fold(g1 * us[layer, part, :].astype(f32))
+                    dvr[part, :] = (vec[1:2] * g1).astype(bf16)
+                    z2[part, :] = mixer_input(kind, low, xs[layer, part, :].astype(f32), vec)
+                mix_grad = mix_grad + nt(dvr[span, :], z2[span, :])
+                product = nn(tams[kind][layer], dvr[span, :])
+                for low, count in blocks(kind):
+                    part = pl.ds(start + low, count)
+                    dz = product[low : low + count]
+                    if low + count > width:
+                        dz = jnp.where(rows_from(low, dz.shape) < width, dz, 0.0)
+                    sums[0] = sums[0] + fold(xs[layer, part, :].astype(f32) * dz)
+                    sums[1] = sums[1] + fold(dz)
+                    grad[part, :] = (grad[part, :].astype(f32) + vec[0:1] * dz).astype(bf16)
             pad[0:rows_k, 0:rows_k] = mix_grad
             if kind == KINDS - 1:
                 for place in range(5):
-                    pad[width + place : width + place + 1, :] = sums[place]
+                    pad[width + place : width + place + 1, :] = col_sum(sums[place])
                 pad[width + 5 : width + 6, :] = (col_sum(vecs[...]) + vec[6:7] * bias_sum) / vec[3:4]
                 pad[width + 6 : width + 7, :] = bias_sum
                 for place in range(plan.hid // chans):
@@ -534,12 +555,14 @@
         functools.partial(unpack, plan),
         out_shape=finals,
         in_specs=[vmem] * 7,
-        out_specs=[anywhere] * 6 + [vmem] * 6 + [anywhere, vmem, anywhere],
+        out_specs=[anywhere] * 6 + [vmem] * 2 + [anywhere] * 3 + [vmem, anywhere, vmem, anywhere],
         scratch_shapes=[
             pltpu.VMEM((LAYERS, chans, hid), f32),
             pltpu.VMEM((LAYERS, hid, chans), f32),
-            pltpu.VMEM((max(plan.wide), chans), f32),
+            pltpu.VMEM((LAYERS, max(plan.wide), chans), f32),
+            *(pltpu.VMEM((width, LAYERS, width), f32) for width in plan.widths),
             pltpu.SemaphoreType.DMA((6,)),
+            pltpu.SemaphoreType.DMA((KINDS,)),
             pltpu.SemaphoreType.DMA((LAYERS, plan.chunks, 2)),
         ],
         compiler_params=pltpu.CompilerParams(vmem_limit_bytes=24 * 1024 * 1024),
@@ -551,48 +574,51 @@
 def unpack(
     plan, ia, ib, ic, ja, jb, jc, held,
     oa, ob, oc, ga, gb, gc, g_scales, g_shifts, g_mix_a, g_mix_b, g_mix_c, g_patch, g_in, g_bias, g_out,
-    wide_in, wide_out, square, copy_sem, out_sem,
+    wide_in, wide_out, square, mix_a, mix_b, mix_c, copy_sem, mix_sem, out_sem,
 ):
     chans, chunks = plan.chans, plan.chunks
     moves = []
     for place, (source, target) in enumerate(zip((ia, ib, ic, ja, jb, jc), (oa, ob, oc, ga, gb, gc))):
         moves.append(pltpu.make_async_copy(source, target, copy_sem.at[place]))
+    for move in moves:
+        move.start()
     g_patch[...] = jnp.zeros_like(g_patch)
+    firsts = [(LAYERS - 1 - layer) * plan.steps for layer in range(LAYERS)]
+    offset = 0
+    for kind, (stage, target) in enumerate(zip((mix_a, mix_b, mix_c), (g_mix_a, g_mix_b, g_mix_c))):
+        width, rows_k, size = plan.widths[kind], plan.padded[kind], plan.wide[kind]
+        for layer in range(LAYERS):
+            for part in range(size // LANES):
+                spot = pl.ds(plan.places[kind] + part * rows_k, rows_k)
+                value = held[firsts[layer] + chunks, spot, :].astype(f32)
+                square[layer, 0:rows_k, part * LANES : (part + 1) * LANES] = value
+            whole = square[layer, 0:rows_k, 0:size]
+            stage[:, layer, :] = whole[0:width, 0:width]
+            row = lax.broadcasted_iota(jnp.int32, (rows_k, size), 0)
+            col = lax.broadcasted_iota(jnp.int32, (rows_k, size), 1)
+            column = jnp.sum(jnp.where(col == width, whole, 0.0), axis=1, keepdims=True)
+            turned = jnp.sum(jnp.where((row == col) & (row < width), column, 0.0), axis=0, keepdims=True)
+            g_patch[layer : layer + 1, offset : offset + width] = turned[:, 0:width]
+        moves.append(pltpu.make_async_copy(stage, target, mix_sem.at[kind]))
+        moves[-1].start()
+        offset += width
     for layer in reversed(range(LAYERS)):
-        if layer == 0:
-            for move in moves[:6]:
-                move.start()
-        first = (LAYERS - 1 - layer) * plan.steps
         for step in range(chunks):
             lanes = pl.ds(step * CHUNK, CHUNK)
+            piece = firsts[layer] + step
             for part in range(CHUNK // LANES):
                 spot = pl.ds(step * CHUNK + part * LANES, LANES)
-                wide_in[layer, :, spot] = held[first + step, pl.ds(part * chans, chans), :].astype(f32)
+                wide_in[layer, :, spot] = held[piece, pl.ds(part * chans, chans), :].astype(f32)
             for part in range(chans // LANES):
                 spot = pl.ds(part * LANES, LANES)
-                wide_out[layer, lanes, spot] = held[first + step, pl.ds(plan.half + part * CHUNK, CHUNK), :].astype(f32)
+                wide_out[layer, lanes, spot] = held[piece, pl.ds(plan.half + part * CHUNK, CHUNK), :].astype(f32)
             for place, (source, target) in enumerate(
                 ((wide_in.at[layer, :, lanes], g_in.at[layer, :, lanes]), (wide_out.at[layer, lanes], g_out.at[layer, lanes]))
             ):
                 moves.append(pltpu.make_async_copy(source, target, out_sem.at[layer, step, place]))
                 moves[-1].start()
-        offset = 0
-        for kind, target in enumerate((g_mix_a, g_mix_b, g_mix_c)):
-            width, rows_k, size = plan.widths[kind], plan.padded[kind], plan.wide[kind]
-            for part in range(size // LANES):
-                place = plan.places[kind] + part * rows_k
-                square[0:rows_k, part * LANES : (part + 1) * LANES] = held[first + chunks, pl.ds(place, rows_k), :].astype(
-                    f32
-                )
-            whole = square[0:rows_k, 0:size]
-            target[:, layer, :] = whole[0:width, 0:width]
-            row = lax.broadcasted_iota(jnp.int32, (rows_k, size), 0)
-            col = lax.broadcasted_iota(jnp.int32, (rows_k, size), 1)
-            column = jnp.sum(jnp.where(col == width, whole, 0.0), axis=1, keepdims=True)
-            turned = jnp.sum(jnp.where((row == col) & (row < width), column, 0.0), axis=0, keepdims=True)
-            g_patch[layer : layer + 1, offset : offset + width] = turned[:, 0:width]
-            offset += width
-        small = square[width : width + 7 + plan.hid // chans, :]
+        width = plan.widths[KINDS - 1]
+        small = square[layer, width : width + 7 + plan.hid // chans, :]
         for place, row in enumerate((0, 2, 3, 5)):
             g_scales[layer, place : place + 1, :] = small[row : row + 1]
         for place, row in enumerate((1, 4, 6)):

time: 94.7 us -> 92.2 us (0.974)
  Pallas kernels: 93.7 us -> 91.2 us
    pallas_call x1, Pallas kernels: 87.6 us -> 85.1 us  [body(): pl.pallas_call(functools.partial(kernel, plan), out_shape=out_shape, in_s...]
where the time goes in v2:
time: 92.2 us; the launch traced here: 92 us
  Pallas kernels  91.2 us (99%)
    pallas_call x1, Pallas kernels, body(): pl.pallas_call(functools.partial(kernel, plan), out_shape=out_shape, in_s...  85.1 us
    pallas_call x1, Pallas kernels, body(): pl.pallas_call(functools.partial(unpack, plan), out_shape=finals, in_spec...  6.08 us

profile of v2, /device:TPU:0, one launch (start us, length us, event | category | flops | bytes accessed | tf_op | source)
XLA Modules:
  0.0 92.0 jit_solution(18080233585205031618)
XLA Ops:
  0.7 85.1 %shard_map.271 = (bf16[100,2,384]{2,1,0:T(2,128)(2,1)S(1)}, bf16[196,2,384]{2,1,0:T(2,128)(2,1)S(1)}, bf16[324,2,384]{2,1,0:T(2,128)(2,1)S(1)}, bf16[100,2,384]{...) custom-call(bf16[100,8,384]{2,1,0:T(8,128)(2,1)} %bitcast.24, ...), custom_call_target="tpu_custom_call" | custom-call | tf_op jit(solution)/shard_map/pallas_call | solution.py:533
  85.8 6.1 %shard_map.272 = (bf16[100,2,384]{2,1,0:T(2,128)(2,1)}, bf16[196,2,384]{2,1,0:T(2,128)(2,1)}, bf16[324,2,384]{2,1,0:T(2,128)(2,1)}, bf16[100,2,384]{2,1,0:T(2,12...) custom-call(bf16[100,2,384]{2,1,0:T(2,128)(2,1)S(1)} %get-tuple-elem, ...), custom_call_target="tpu_custom_call" | custom-call | tf_op jit(solution)/shard_map/pallas_call | solution.py:554

commit v3 on v2

--- a/solution.py
+++ b/solution.py
@@ -170,6 +170,19 @@
     def fold(value):
         return value.reshape(-1, 8, chans).sum(axis=0)
 
+    def hidden(layer, chunk, begin, start, size):
+        lanes = pl.ds(begin, CHUNK)
+        bias = bias32[layer, :, lanes]
+        product = nn(z2[pl.ds(start, size), :], w_in[layer, :, lanes])
+        for low in range(0, size, BLOCK):
+            high = min(low + BLOCK, size)
+            a = product[low:high] + bias
+            cdf = 0.5 + 0.5 * lax.erf(a * HALF_ROOT)
+            slope = a * jnp.exp2(a * a * HALF_LOG2E) * PDF_SCALE
+            part = pl.ds(start + low, high - low)
+            hs[layer, chunk, part, :] = (a * cdf).astype(bf16)
+            ds[layer, chunk, part, :] = (cdf + slope).astype(bf16)
+
     def forward(layer):
         vec = aff[layer]
         for kind, slot, start in plan.segments:
@@ -192,29 +205,18 @@
             fetches[6].wait()
             fetches[7].wait()
 
+        if layer == LAYERS - 1:
+            return
         for chunk in range(plan.chunks):
-            lanes = pl.ds(chunk * CHUNK, CHUNK)
-            bias = bias32[layer, :, lanes]
-            first_weight = w_in[layer, :, lanes]
-            second_weight = w_out[layer, lanes, :]
+            second_weight = w_out[layer, pl.ds(chunk * CHUNK, CHUNK), :]
             for start, size in cuts(rows, 4):
                 span = pl.ds(start, size)
-                product = nn(z2[span, :], first_weight)
-                for low in range(0, size, BLOCK):
-                    high = min(low + BLOCK, size)
-                    a = product[low:high] + bias
-                    cdf = 0.5 + 0.5 * lax.erf(a * HALF_ROOT)
-                    slope = a * jnp.exp2(a * a * HALF_LOG2E) * PDF_SCALE
-                    block_span = pl.ds(start + low, high - low)
-                    hs[layer, chunk, block_span, :] = (a * cdf).astype(bf16)
-                    ds[layer, chunk, block_span, :] = (cdf + slope).astype(bf16)
-                if layer < LAYERS - 1:
-                    acc[span, :] += nn(hs[layer, chunk, span, :], second_weight)
-
-        if layer < LAYERS - 1:
-            for kind, slot, start in plan.segments:
-                span = pl.ds(start, padded[kind])
-                xs[layer + 1, span, :] = (x1s[layer, span, :].astype(f32) + vec[3:4] * acc[span, :]).astype(bf16)
+                hidden(layer, chunk, chunk * CHUNK, start, size)
+                acc[span, :] += nn(hs[layer, chunk, span, :], second_weight)
+
+        for kind, slot, start in plan.segments:
+            span = pl.ds(start, padded[kind])
+            xs[layer + 1, span, :] = (x1s[layer, span, :].astype(f32) + vec[3:4] * acc[span, :]).astype(bf16)
 
     for layer in range(LAYERS):
         forward(layer)
@@ -362,6 +364,8 @@
             total = jnp.zeros((8, CHUNK), f32)
             for start, size in cuts(rows, 4):
                 span = pl.ds(start, size)
+                if layer == LAYERS - 1:
+                    hidden(layer, chunk, pl.multiple_of(chunk * CHUNK, CHUNK), start, size)
                 dh = nt(dvr[span, :], second_weight)
                 for low in range(0, size, BLOCK):
                     high = min(low + BLOCK, size)

time: 92.2 us -> 93.7 us (1.016)
  Pallas kernels: 91.2 us -> 92.7 us
    pallas_call x1, Pallas kernels: 85.1 us -> 86.6 us  [body(): pl.pallas_call(functools.partial(kernel, plan), out_shape=out_shape, in_s...]
where the time goes in v3:
time: 93.7 us; the launch traced here: 93.6 us
  Pallas kernels  92.7 us (99%)
    pallas_call x1, Pallas kernels, body(): pl.pallas_call(functools.partial(kernel, plan), out_shape=out_shape, in_s...  86.6 us
    pallas_call x1, Pallas kernels, body(): pl.pallas_call(functools.partial(unpack, plan), out_shape=finals, in_spec...  6.08 us

profile of v3, /device:TPU:0, one launch (start us, length us, event | category | flops | bytes accessed | tf_op | source)
XLA Modules:
  0.0 93.6 jit_solution(15960530086325849374)
XLA Ops:
  0.7 86.6 %shard_map.271 = (bf16[100,2,384]{2,1,0:T(2,128)(2,1)S(1)}, bf16[196,2,384]{2,1,0:T(2,128)(2,1)S(1)}, bf16[324,2,384]{2,1,0:T(2,128)(2,1)S(1)}, bf16[100,2,384]{...) custom-call(bf16[100,8,384]{2,1,0:T(8,128)(2,1)} %bitcast.24, ...), custom_call_target="tpu_custom_call" | custom-call | tf_op jit(solution)/shard_map/pallas_call | solution.py:537
  87.3 6.1 %shard_map.272 = (bf16[100,2,384]{2,1,0:T(2,128)(2,1)}, bf16[196,2,384]{2,1,0:T(2,128)(2,1)}, bf16[324,2,384]{2,1,0:T(2,128)(2,1)}, bf16[100,2,384]{2,1,0:T(2,12...) custom-call(bf16[100,2,384]{2,1,0:T(2,128)(2,1)S(1)} %get-tuple-elem, ...), custom_call_target="tpu_custom_call" | custom-call | tf_op jit(solution)/shard_map/pallas_call | solution.py:558

commit v4 on v1

--- a/solution.py
+++ b/solution.py
@@ -15,7 +15,7 @@
 LANES = 128
 ROWS = 16
 CHUNK = 256
-SLACK = 2
+DELAYS = (0, 1, 3, 5, 7, 9, 11, 13, 14)
 BLOCK = 32
 HALF_LOG2E = -0.7213475204444817
 HALF_ROOT = 0.7071067811865476
@@ -182,7 +182,7 @@
             bias = bias32[layer, :, lanes]
             first_weight = w_in[layer, :, lanes]
             second_weight = w_out[layer, lanes, :]
-            for start, size in cuts(rows, 2):
+            for start, size in cuts(rows, 4):
                 span = pl.ds(start, size)
                 product = nn(z2[span, :], first_weight)
                 for low in range(0, size, BLOCK):
@@ -314,7 +314,7 @@
 
     def tick(moment):
         for stage in range(len(hops) + 1):
-            piece = moment - SLACK * stage
+            piece = moment - DELAYS[stage]
 
             @pl.when((piece >= 0) & (piece < plan.pieces))
             def _(stage=stage, piece=piece):
@@ -345,7 +345,7 @@
             first_weight = w_in[layer, :, lanes]
             second_weight = w_out[layer, lanes, :]
             total = jnp.zeros((8, CHUNK), f32)
-            for start, size in cuts(rows, 1):
+            for start, size in cuts(rows, 4):
                 span = pl.ds(start, size)
                 dh = nt(dvr[span, :], second_weight)
                 for low in range(0, size, BLOCK):
@@ -439,7 +439,7 @@
 
         return carry
 
-    lax.fori_loop(plan.pieces, plan.pieces + SLACK * len(hops), drain, 0)
+    lax.fori_loop(plan.pieces, plan.pieces + DELAYS[-1], drain, 0)
 
     for hop, total in enumerate(totals):
         pltpu.make_async_remote_copy(

time: 94.7 us -> 89.1 us (0.941)
  Pallas kernels: 93.7 us -> 88.1 us
    pallas_call x1, Pallas kernels: 87.6 us -> 82 us  [body(): pl.pallas_call(functools.partial(kernel, plan), out_shape=out_shape, in_s...]
where the time goes in v4:
time: 89.1 us; the launch traced here: 89 us
  Pallas kernels  88.1 us (99%)
    pallas_call x1, Pallas kernels, body(): pl.pallas_call(functools.partial(kernel, plan), out_shape=out_shape, in_s...  82 us
    pallas_call x1, Pallas kernels, body(): pl.pallas_call(functools.partial(unpack, plan), out_shape=finals, in_spec...  6.17 us

profile of v4, /device:TPU:0, one launch (start us, length us, event | category | flops | bytes accessed | tf_op | source)
XLA Modules:
  0.0 89.0 jit_solution(2838966686704785262)
XLA Ops:
  0.7 82.0 %shard_map.271 = (bf16[100,2,384]{2,1,0:T(2,128)(2,1)S(1)}, bf16[196,2,384]{2,1,0:T(2,128)(2,1)S(1)}, bf16[324,2,384]{2,1,0:T(2,128)(2,1)S(1)}, bf16[100,2,384]{...) custom-call(bf16[100,8,384]{2,1,0:T(8,128)(2,1)} %bitcast.24, ...), custom_call_target="tpu_custom_call" | custom-call | tf_op jit(solution)/shard_map/pallas_call | solution.py:512
  82.6 6.2 %shard_map.272 = (bf16[100,2,384]{2,1,0:T(2,128)(2,1)}, bf16[196,2,384]{2,1,0:T(2,128)(2,1)}, bf16[324,2,384]{2,1,0:T(2,128)(2,1)}, bf16[100,2,384]{2,1,0:T(2,12...) custom-call(bf16[100,2,384]{2,1,0:T(2,128)(2,1)S(1)} %get-tuple-elem, ...), custom_call_target="tpu_custom_call" | custom-call | tf_op jit(solution)/shard_map/pallas_call | solution.py:533
